TPU v7x, 32 devices: a whole 2x2x4 slice. The times are simulated.
32 devices in a mesh: seqa: 8 (over z, y), seqb: 4 (over x, core).
Axes of the slice: x: 2, y: 2, z: 4, core: 2. Of those that a mesh axis runs over, the one named last changes fastest.
Arguments:
- query_rows: bfloat16 [8192, 768], P(('seqa', 'seqb')), may hold values from -16 to 16
- key_rows: bfloat16 [8192, 768], P(('seqa', 'seqb')), may hold values from -16 to 16
- value_rows: bfloat16 [8192, 768], P(('seqa', 'seqb')), may hold values from -5.5 to 5.5
Outputs:
- attended: bfloat16 [8192, 768], P(('seqa', 'seqb'))
All inputs are finite; a program needn't handle non-finite values.
Results may differ from a plain program's by a relative error of at most 0.0028.
Values may be sent and summed in bfloat16 or wider, within the bound.
A program may use at most 64 MiB of HBM per device.

v0:
```python
import math

import jax
import jax.numpy as jnp
from jax import lax
from jax.sharding import PartitionSpec as P

HEADS = 12
BLOCK = 128


LOG_TWO = math.log(2.0)
HIGHEST = lax.Precision.HIGHEST


def passed_along(block, axis, distance):
    devices = range(lax.axis_size(axis))
    route = [(i - distance, i) for i in devices if i - distance in devices]
    return lax.ppermute(block, axis, route)


def from_partner(value, axis, bit):
    mask = 2**bit
    pairs = [(source, source ^ mask) for source in range(lax.axis_size(axis))]
    return lax.ppermute(value, axis, pairs)


def halve_rows(matrix):
    amount, features = matrix.shape
    paired = matrix.reshape(amount // 2, 2, features).astype(jnp.float32)
    return 0.5 * (paired[:, 0] + paired[:, 1])


def coarse_terms(
    queries, halves, left_keys, right_keys, left_values, right_values, left_ok, right_ok, height
):
    batches, amount, features = queries.shape
    width = left_keys.shape[1]
    head_dim = features // HEADS
    query_heads = queries.reshape(batches, amount, HEADS, head_dim)
    key_heads = jnp.concatenate([left_keys, right_keys], axis=1).reshape(
        batches, 2 * width, HEADS, head_dim
    )
    value_heads = jnp.concatenate([left_values, right_values], axis=1).reshape(
        batches, 2 * width, HEADS, head_dim
    )
    scores = jnp.einsum("bqhe,bkhe->bhqk", query_heads, key_heads, precision=HIGHEST)
    logits = scores * head_dim ** (-0.5) + height * LOG_TWO
    key_half = jnp.arange(width) >= width // 2
    query_half = halves[:, :, None]
    keep_left = (query_half | jnp.logical_not(key_half)[None, None, :]) & left_ok[:, None, None]
    keep_right = (key_half[None, None, :] | jnp.logical_not(query_half)) & right_ok[:, None, None]
    allowed = jnp.concatenate([keep_left, keep_right], axis=2)[:, None]
    logits = jnp.where(allowed, logits, -jnp.inf)
    highest = jnp.max(logits, axis=3)
    weights = jnp.exp(logits - highest[..., None])
    totals = jnp.sum(weights, axis=3)
    output = jnp.einsum("bhqk,bkhe->bqhe", weights, value_heads, precision=HIGHEST)
    return (jnp.swapaxes(highest, 1, 2), jnp.swapaxes(totals, 1, 2), output)


def flatten(level_terms):
    return tuple((part.reshape((-1,) + part.shape[2:]) for part in level_terms))


def merge_terms(earlier, later):
    highest = jnp.maximum(earlier[0], later[0])
    scale_one = jnp.exp(earlier[0] - highest)
    scale_two = jnp.exp(later[0] - highest)
    totals = scale_one * earlier[1] + scale_two * later[1]
    output = scale_one[..., None] * earlier[2] + scale_two[..., None] * later[2]
    return (highest, totals, output)


def widen(combined):
    return tuple((jnp.repeat(part, 2, axis=0) for part in combined))


def deep_terms(
    own_queries,
    below_keys,
    above_keys,
    below_values,
    above_values,
    position,
    spread,
    block_total,
    height,
):
    amount = own_queries.shape[0]
    block_index = position // spread
    offset = position % spread * amount
    halves = offset + jnp.arange(amount) >= BLOCK // 2
    left_ok = block_index > 0
    right_ok = block_index < block_total - 1
    level_terms = coarse_terms(
        own_queries[None],
        halves[None],
        below_keys[None],
        above_keys[None],
        below_values[None],
        above_values[None],
        left_ok[None],
        right_ok[None],
        height,
    )
    return flatten(level_terms)


def fine_terms(queries, keys_window, values_window, left_ok, right_ok, coarse):
    per_group, amount, heads, head_dim = queries.shape
    scores = jnp.einsum(
        "bqhe,bkhe->bhqk", queries, keys_window, preferred_element_type=jnp.float32
    ) * head_dim ** (-0.5)
    section = jnp.arange(3 * amount) // amount
    allowed = ((section != 0)[None, :] | left_ok[:, None]) & (
        (section != 2)[None, :] | right_ok[:, None]
    )
    scores = jnp.where(allowed[:, None, None, :], scores, -jnp.inf)
    highest = jnp.max(scores, axis=3)
    weights = jnp.exp(scores - highest[..., None])
    totals = jnp.sum(weights, axis=3)
    output = jnp.einsum(
        "bhqk,bkhe->bqhe",
        weights.astype(jnp.bfloat16),
        values_window,
        preferred_element_type=jnp.float32,
    )
    fine = (jnp.swapaxes(highest, 1, 2), jnp.swapaxes(totals, 1, 2), output)
    widened = tuple(
        (
            jnp.repeat(part, 2, axis=0).reshape((per_group, amount) + part.shape[1:])
            for part in coarse
        )
    )
    merged = merge_terms(fine, widened)
    result = merged[2] / merged[1][..., None]
    return result.reshape(per_group * amount, heads * head_dim).astype(jnp.bfloat16)


def shards(query_rows, key_rows, value_rows):
    length, features = query_rows.shape
    head_dim = features // HEADS
    inner_size = lax.axis_size("seqb")
    devices = lax.axis_size("seqa") * inner_size
    position = lax.axis_index("seqa") * inner_size + lax.axis_index("seqb")
    is_first = position == 0
    is_last = position == devices - 1
    local_levels = (length // BLOCK).bit_length() - 1
    top_level = local_levels + devices.bit_length() - 2
    lower_fine = passed_along(
        (key_rows[length - BLOCK :], value_rows[length - BLOCK :]), ("seqa", "seqb"), 1
    )
    upper_fine = passed_along((key_rows[:BLOCK], value_rows[:BLOCK]), ("seqa", "seqb"), -1)
    levels_q, levels_k, levels_v = ([], [], [])
    lower_rims, upper_rims = ([], [])
    coarse_query, coarse_key, coarse_value = (query_rows, key_rows, value_rows)
    coarse_query = halve_rows(coarse_query)
    coarse_key = halve_rows(coarse_key)
    coarse_value = halve_rows(coarse_value)
    levels_q.append(coarse_query)
    levels_k.append(coarse_key)
    levels_v.append(coarse_value)
    lower_rims.append(
        (
            passed_along(coarse_key.astype(jnp.bfloat16), ("seqa", "seqb"), 1).astype(
                coarse_key.dtype
            ),
            passed_along(coarse_value.astype(jnp.bfloat16), ("seqa", "seqb"), 1).astype(
                coarse_value.dtype
            ),
        )
    )
    upper_rims.append(passed_along((coarse_key, coarse_value), ("seqa", "seqb"), -1))
    results = {}
    height = 1
    amount = levels_q[height - 1].shape[0]
    blocks = amount // BLOCK
    ext_key = jnp.concatenate(
        [lower_rims[height - 1][0], levels_k[height - 1], upper_rims[height - 1][0]]
    ).reshape(blocks + 2, BLOCK, features)
    ext_value = jnp.concatenate(
        [lower_rims[height - 1][1], levels_v[height - 1], upper_rims[height - 1][1]]
    ).reshape(blocks + 2, BLOCK, features)
    block_ids = jnp.arange(blocks)
    left_ok = (block_ids > 0) | jnp.logical_not(is_first)
    right_ok = (block_ids < blocks - 1) | jnp.logical_not(is_last)
    halves = jnp.broadcast_to(jnp.arange(BLOCK) >= BLOCK // 2, (blocks, BLOCK))
    level_terms = coarse_terms(
        levels_q[height - 1].reshape(blocks, BLOCK, features),
        halves,
        ext_key[:-2],
        ext_key[2:],
        ext_value[:-2],
        ext_value[2:],
        left_ok,
        right_ok,
        height,
    )
    results[height] = flatten(level_terms)
    group_key, group_value = (levels_k[-1], levels_v[-1])
    own_queries = levels_q[-1]
    for height in range(local_levels + 1, top_level + 1):
        step_bits = height - local_levels
        spread = 2**step_bits
        half_key = halve_rows(group_key)
        half_value = halve_rows(group_value)
        other_key, other_value = (
            from_partner(half_key.astype(jnp.bfloat16), ("seqa", "seqb"), step_bits - 1).astype(
                half_key.dtype
            ),
            from_partner(half_value.astype(jnp.bfloat16), ("seqa", "seqb"), step_bits - 1).astype(
                half_value.dtype
            ),
        )
        upper_half = position // (spread // 2) % 2 == 1
        group_key = jnp.where(
            upper_half,
            jnp.concatenate([other_key, half_key]),
            jnp.concatenate([half_key, other_key]),
        )
        group_value = jnp.where(
            upper_half,
            jnp.concatenate([other_value, half_value]),
            jnp.concatenate([half_value, other_value]),
        )
        below_key, below_value = (
            passed_along(group_key.astype(jnp.bfloat16), ("seqa", "seqb"), spread).astype(
                group_key.dtype
            ),
            passed_along(group_value.astype(jnp.bfloat16), ("seqa", "seqb"), spread).astype(
                group_value.dtype
            ),
        )
        above_key, above_value = (
            passed_along(group_key.astype(jnp.bfloat16), ("seqa", "seqb"), -spread).astype(
                group_key.dtype
            ),
            passed_along(group_value.astype(jnp.bfloat16), ("seqa", "seqb"), -spread).astype(
                group_value.dtype
            ),
        )
        own_queries = halve_rows(own_queries)
        results[height] = deep_terms(
            own_queries,
            below_key,
            above_key,
            below_value,
            above_value,
            position,
            spread,
            devices // spread,
            height,
        )
    combined = results[top_level]
    for height in range(top_level - 1, 0, -1):
        combined = merge_terms(widen(combined), results[height])
    blocks = length // BLOCK
    ext_key = jnp.concatenate([lower_fine[0], key_rows, upper_fine[0]]).reshape(
        blocks + 2, BLOCK, HEADS, head_dim
    )
    ext_value = jnp.concatenate([lower_fine[1], value_rows, upper_fine[1]]).reshape(
        blocks + 2, BLOCK, HEADS, head_dim
    )
    window_key = jnp.concatenate([ext_key[:-2], ext_key[1:-1], ext_key[2:]], axis=1)
    window_value = jnp.concatenate([ext_value[:-2], ext_value[1:-1], ext_value[2:]], axis=1)
    per_group = min(4, blocks)
    group_count = blocks // per_group
    block_ids = jnp.arange(blocks)
    left_ok = ((block_ids > 0) | jnp.logical_not(is_first)).reshape(group_count, per_group)
    right_ok = ((block_ids < blocks - 1) | jnp.logical_not(is_last)).reshape(group_count, per_group)
    grouped_queries = query_rows.reshape(group_count, per_group, BLOCK, HEADS, head_dim)
    grouped_keys = window_key.reshape((group_count, per_group) + window_key.shape[1:])
    grouped_values = window_value.reshape((group_count, per_group) + window_value.shape[1:])
    grouped_coarse = tuple(
        (part.reshape((group_count, per_group * BLOCK // 2) + part.shape[1:]) for part in combined)
    )

    def fine_group(inputs):
        return fine_terms(inputs[0], inputs[1], inputs[2], inputs[3], inputs[4], inputs[5])

    pieces = lax.map(
        fine_group,
        (grouped_queries, grouped_keys, grouped_values, left_ok, right_ok, grouped_coarse),
    )
    return pieces.reshape(length, features)


def solution(mesh):
    placed = (P(("seqa", "seqb"), None), P(("seqa", "seqb"), None), P(("seqa", "seqb"), None))
    return jax.shard_map(
        shards, mesh=mesh, in_specs=placed, out_specs=P(("seqa", "seqb"), None), check_vma=False
    )
```

profile of v0, /device:TPU:0, one launch (start us, length us, event | category | flops | bytes accessed | tf_op | source)
XLA Modules:
  0.0 278.0 jit_solution(266423562735571180)
XLA Ops:
  0.0 1.8 fusion.187
  1.8 3.1 %collective-permute-start = (bf16[128,768]{1,0:T(8,128)(2,1)}, bf16[128,768]{1,0:T(8,128)(2,1)}, u32[]{:S(2)}, u32[]{:S(2)}) collective-permute-start(bf16[128,768]{1,0:T(8,128)(2,1)} %get-tuple-element.88), channel_id=1, source_target_pairs={{0,1},{1,2},{2,3},{3,4},{4,5},{5,6},{6,7},{7,8},{8,9},{9,10},{10,1... | collective-permute-start | bytes 589832 | tf_op jit(solution)/shard_map/ppermute | solution.py:19
  6.1 1.8 fusion.186
  7.9 5.2 %collective-permute-start.16 = (bf16[128,768]{1,0:T(8,128)(2,1)}, bf16[128,768]{1,0:T(8,128)(2,1)}, u32[]{:S(2)}, u32[]{:S(2)}) collective-permute-start(bf16[128,768]{1,0:T(8,128)(2,1)} %get-tuple-element.84), channel_id=1, source_target_pairs={{0,1},{1,2},{2,3},{3,4},{4,5},{5,6},{6,7},{7,8},{8,9},{9,10},{10,1... | collective-permute-start | bytes 589832 | tf_op jit(solution)/shard_map/ppermute | solution.py:19
  18.6 1.7 collective-permute-start.2
  21.2 2.1 fusion.175
  30.9 2.1 fusion.173
  46.1 2.5 collective-permute-start.3
  50.5 1.6 collective-permute-done.3
  52.0 2.5 collective-permute-start.14
  57.2 3.8 %collective-permute-start.19 = (bf16[64,768]{1,0:T(8,128)(2,1)}, bf16[64,768]{1,0:T(8,128)(2,1)}, u32[]{:S(2)}, u32[]{:S(2)}) collective-permute-start(bf16[64,768]{1,0:T(8,128)(2,1)} %bitcast.336), channel_id=1, source_target_pairs={{0,2},{1,3},{2,0},{3,1},{4,6},{5,7},{6,4},{7,5},{8,10},{9,11},{10,... | collective-permute-start | bytes 294920 | tf_op jit(solution)/shard_map/ppermute | solution.py:25
  64.2 4.8 %collective-permute-done.19 = bf16[64,768]{1,0:T(8,128)(2,1)} collective-permute-done((bf16[64,768]{1,0:T(8,128)(2,1)}, bf16[64,768]{1,0:T(8,128)(2,1)}, u32[]{:S(2)}, u32[]{:S(2)}) %collective-permute-start.19) | collective-permute-done | bytes 98336 | tf_op jit(solution)/shard_map/ppermute | solution.py:25
  72.9 2.4 bitcast_reduce_fusion
  75.3 2.1 fusion.1
  79.0 6.4 %collective-permute-start.4 = (bf16[64,768]{1,0:T(8,128)(2,1)}, bf16[64,768]{1,0:T(8,128)(2,1)S(1)}, u32[]{:S(2)}, u32[]{:S(2)}) collective-permute-start(bf16[64,768]{1,0:T(8,128)(2,1)} %get-tuple-element.52), channel_id=1, source_target_pairs={{0,4},{1,5},{2,6},{3,7},{4,0},{5,1},{6,2},{7,3},{8,12},{9,13},{10,... | collective-permute-start | bytes 294920 | tf_op jit(solution)/shard_map/ppermute | solution.py:25
  91.1 5.2 %collective-permute-start.12 = (bf16[128,768]{1,0:T(8,128)(2,1)}, bf16[128,768]{1,0:T(8,128)(2,1)}, u32[]{:S(2)}, u32[]{:S(2)}) collective-permute-start(bf16[128,768]{1,0:T(8,128)(2,1)} %get-tuple-element.68), channel_id=1, source_target_pairs={{0,2},{1,3},{2,4},{3,5},{4,6},{5,7},{6,8},{7,9},{8,10},{9,11},{10,... | collective-permute-start | bytes 589832 | tf_op jit(solution)/shard_map/ppermute | solution.py:19
  97.5 4.5 %collective-permute-done.20 = bf16[64,768]{1,0:T(8,128)(2,1)} collective-permute-done((bf16[64,768]{1,0:T(8,128)(2,1)S(1)}, bf16[64,768]{1,0:T(8,128)(2,1)}, u32[]{:S(2)}, u32[]{:S(2)}) %collective-permute-start.20) | collective-permute-done | bytes 98336 | tf_op jit(solution)/shard_map/ppermute | solution.py:25
  105.2 5.2 %collective-permute-start.28 = (bf16[128,768]{1,0:T(8,128)(2,1)}, bf16[128,768]{1,0:T(8,128)(2,1)}, u32[]{:S(2)}, u32[]{:S(2)}) collective-permute-start(bf16[128,768]{1,0:T(8,128)(2,1)} %get-tuple-element.62), channel_id=1, source_target_pairs={{0,2},{1,3},{2,4},{3,5},{4,6},{5,7},{6,8},{7,9},{8,10},{9,11},{10,... | collective-permute-start | bytes 589832 | tf_op jit(solution)/shard_map/ppermute | solution.py:19
  112.2 1.7 copy.287
  113.9 1.6 fusion.189
  116.5 5.2 %collective-permute-start.10 = (bf16[128,768]{1,0:T(8,128)(2,1)}, bf16[128,768]{1,0:T(8,128)(2,1)}, u32[]{:S(2)}, u32[]{:S(2)}) collective-permute-start(bf16[128,768]{1,0:T(8,128)(2,1)} %get-tuple-element.56), channel_id=1, source_target_pairs={{0,4},{1,5},{2,6},{3,7},{4,8},{5,9},{6,10},{7,11},{8,12},{9,13},{1... | collective-permute-start | bytes 589832 | tf_op jit(solution)/shard_map/ppermute | solution.py:19
  121.7 1.7 copy.318
  124.7 1.8 copy.317
  128.1 5.3 %collective-permute-start.26 = (bf16[128,768]{1,0:T(8,128)(2,1)}, bf16[128,768]{1,0:T(8,128)(2,1)}, u32[]{:S(2)}, u32[]{:S(2)}) collective-permute-start(bf16[128,768]{1,0:T(8,128)(2,1)} %get-tuple-element.60), channel_id=1, source_target_pairs={{0,4},{1,5},{2,6},{3,7},{4,8},{5,9},{6,10},{7,11},{8,12},{9,13},{1... | collective-permute-start | bytes 589832 | tf_op jit(solution)/shard_map/ppermute | solution.py:19
  133.4 1.7 copy.283
  135.2 1.7 collective-permute-start.5
  136.8 1.9 copy.294
  138.7 2.7 fusion.188
  144.0 1.5 fusion.190
  146.3 2.6 collective-permute-start.21
  149.0 1.8 fusion.67
  151.8 4.6 %collective-permute-start.8 = (bf16[128,768]{1,0:T(8,128)(2,1)}, bf16[128,768]{1,0:T(8,128)(2,1)}, u32[]{:S(2)}, u32[]{:S(2)}) collective-permute-start(bf16[128,768]{1,0:T(8,128)(2,1)} %get-tuple-element.50), channel_id=1, source_target_pairs={{0,8},{1,9},{2,10},{3,11},{4,12},{5,13},{6,14},{7,15},{8,16},{9,17... | collective-permute-start | bytes 589832 | tf_op jit(solution)/shard_map/ppermute | solution.py:19
  158.4 1.7 copy.315
  160.1 5.5 %collective-permute-start.24 = (bf16[128,768]{1,0:T(8,128)(2,1)}, bf16[128,768]{1,0:T(8,128)(2,1)}, u32[]{:S(2)}, u32[]{:S(2)}) collective-permute-start(bf16[128,768]{1,0:T(8,128)(2,1)} %get-tuple-element.54), channel_id=1, source_target_pairs={{0,8},{1,9},{2,10},{3,11},{4,12},{5,13},{6,14},{7,15},{8,16},{9,17... | collective-permute-start | bytes 589832 | tf_op jit(solution)/shard_map/ppermute | solution.py:19
  165.7 1.8 copy.314
  167.4 1.5 collective-permute-start.7
  171.2 6.6 %collective-permute-start.6 = (bf16[128,768]{1,0:T(8,128)(2,1)}, bf16[128,768]{1,0:T(8,128)(2,1)}, u32[]{:S(2)}, u32[]{:S(2)}) collective-permute-start(bf16[128,768]{1,0:T(8,128)(2,1)} %fusion.67), channel_id=1, source_target_pairs={{0,16},{1,17},{2,18},{3,19},{4,20},{5,21},{6,22},{7,23},{8,24},{9,... | collective-permute-start | bytes 589832 | tf_op jit(solution)/shard_map/ppermute | solution.py:19
  177.8 1.7 copy.278
  180.8 1.8 copy.277
  182.6 2.7 fusion.191
  185.2 6.8 %collective-permute-start.22 = (bf16[128,768]{1,0:T(8,128)(2,1)}, bf16[128,768]{1,0:T(8,128)(2,1)}, u32[]{:S(2)}, u32[]{:S(2)}) collective-permute-start(bf16[128,768]{1,0:T(8,128)(2,1)} %fusion.76), channel_id=1, source_target_pairs={{0,16},{1,17},{2,18},{3,19},{4,20},{5,21},{6,22},{7,23},{8,24},{9,... | collective-permute-start | bytes 589832 | tf_op jit(solution)/shard_map/ppermute | solution.py:19
  192.0 1.7 copy.313
  193.8 1.8 copy.312
  195.5 1.7 fusion.105
  197.2 1.7 copy.274
  199.0 1.8 copy.273
  200.7 2.6 fusion.192
  207.3 1.7 fusion.110
  226.5 1.4 copy.330
  230.7 1.4 copy.290
  236.3 1.5 copy.332
  240.6 1.5 copy.295
  244.9 1.6 broadcast_in_dim.231
  246.4 1.6 copy.334
  249.4 1.6 broadcast_in_dim.221
  251.0 1.6 copy.297
  252.6 1.7 copy.311
  254.3 1.7 copy.310
  256.1 1.6 convolution_bitcast_fusion.3
  257.7 1.6 fusion.47
  259.4 1.5 fusion.43
  262.0 2.6 fusion.25
  266.4 3.4 %fusion.26 = f32[128,12,64]{0,2,1:T(8,128)} fusion(f32[12,128,256]{2,1,0:T(8,128)S(1)} %get-tuple-element.101, f32[1,128,12,64]{1,3,2,0:T(8,128)S(1)} %bitcast.344, f32[1,128,12,64]{1,3,2,0:T(8,128)S(1)} %bitcast.343, f32[12,128]{1,0:T(8,128)S(1)} %get-tuple-element.100, f32[128,12,64]{0,2,1:T(8,128)S(1)} %copy.320, f32[128,12]{0,1:T(8,128)} %get-tuple-element.28, ...), kind=kOutput, calls=%fused_computation.26 | convolution fusion | flops 302874624 | bytes 3164160 | tf_op jit(solution)/shard_map/bhqk,bkhe->bqhe/dot_general | solution.py:58
  272.9 3.6 %fusion.53 = bf16[2,128,12,64]{1,3,2,0:T(8,128)(2,1)S(1)} fusion(f32[2,12,384,128]{3,2,1,0:T(8,128)} %copy-done.2, f32[2,12,128]{2,1,0:T(8,128)S(1)} %copy-done.16, pred[2,384]{1,0:T(4,128)(4,1)} %copy-done.19, bf16[2,128,12,64]{1,3,2,0:T(8,128)(2,1)S(1)} %copy-done.8, bf16[2,128,12,64]{1,3,2,0:T(8,128)(2,1)S(1)} %copy-done.6, ...), kind=kOutput, calls=%fused_computation.55 | convolution fusion | flops 160235520 | bytes 7127808 | tf_op jit(solution)/shard_map/while/body/eval_jaxpr/bhqk,bkhe->bqhe/dot_general | solution.py:123
  (236 shorter events, 109.5 us)
Async XLA Ops:
  1.8 54.0 %collective-permute-start = (bf16[128,768]{1,0:T(8,128)(2,1)}, bf16[128,768]{1,0:T(8,128)(2,1)}, u32[]{:S(2)}, u32[]{:S(2)}) collective-permute-start(bf16[128,768]{1,0:T(8,128)(2,1)} %get-tuple-element.88), channel_id=1, source_target_pairs={{0,1},{1,2},{2,3},{3,4},{4,5},{5,6},{6,7},{7,8},{8,9},{9,10},{10,1... | collective-permute-start | bytes 589832 | tf_op jit(solution)/shard_map/ppermute | solution.py:19
  4.8 52.3 %collective-permute-start.1 = (bf16[128,768]{1,0:T(8,128)(2,1)}, bf16[128,768]{1,0:T(8,128)(2,1)}, u32[]{:S(2)}, u32[]{:S(2)}) collective-permute-start(bf16[128,768]{1,0:T(8,128)(2,1)} %get-tuple-element.89), channel_id=1, source_target_pairs={{1,0},{2,1},{3,2},{4,3},{5,4},{6,5},{7,6},{8,7},{9,8},{10,9},{11,1... | collective-permute-start | bytes 589832 | tf_op jit(solution)/shard_map/ppermute | solution.py:19
  7.9 69.8 %collective-permute-start.16 = (bf16[128,768]{1,0:T(8,128)(2,1)}, bf16[128,768]{1,0:T(8,128)(2,1)}, u32[]{:S(2)}, u32[]{:S(2)}) collective-permute-start(bf16[128,768]{1,0:T(8,128)(2,1)} %get-tuple-element.84), channel_id=1, source_target_pairs={{0,1},{1,2},{2,3},{3,4},{4,5},{5,6},{6,7},{7,8},{8,9},{9,10},{10,1... | collective-permute-start | bytes 589832 | tf_op jit(solution)/shard_map/ppermute | solution.py:19
  13.1 7.2 %copy-start = (bf16[256,768]{1,0:T(8,128)(2,1)S(1)}, bf16[256,768]{1,0:T(8,128)(2,1)}, u32[]{:S(2)}) copy-start(bf16[256,768]{1,0:T(8,128)(2,1)} %param.4) | copy-start | bytes 1179652
  13.1 65.9 %collective-permute-start.17 = (bf16[128,768]{1,0:T(8,128)(2,1)}, bf16[128,768]{1,0:T(8,128)(2,1)}, u32[]{:S(2)}, u32[]{:S(2)}) collective-permute-start(bf16[128,768]{1,0:T(8,128)(2,1)} %get-tuple-element.85), channel_id=1, source_target_pairs={{1,0},{2,1},{3,2},{4,3},{5,4},{6,5},{7,6},{8,7},{9,8},{10,9},{11,1... | collective-permute-start | bytes 589832 | tf_op jit(solution)/shard_map/ppermute | solution.py:19
  15.9 4.6 %copy-start.1 = (bf16[256,768]{1,0:T(8,128)(2,1)S(1)}, bf16[256,768]{1,0:T(8,128)(2,1)}, u32[]{:S(2)}) copy-start(bf16[256,768]{1,0:T(8,128)(2,1)} %param.5) | copy-start | bytes 1179652
  17.3 3.4 %copy-start.3 = (bf16[256,768]{1,0:T(8,128)(2,1)S(1)}, bf16[256,768]{1,0:T(8,128)(2,1)}, u32[]{:S(2)}) copy-start(bf16[256,768]{1,0:T(8,128)(2,1)} %param.3) | copy-start | bytes 1179652
  18.6 25.2 %collective-permute-start.2 = (bf16[64,768]{1,0:T(8,128)(2,1)}, bf16[64,768]{1,0:T(8,128)(2,1)}, u32[]{:S(2)}, u32[]{:S(2)}) collective-permute-start(bf16[64,768]{1,0:T(8,128)(2,1)} %get-tuple-element.70), channel_id=1, source_target_pairs={{0,1},{1,0},{2,3},{3,2},{4,5},{5,4},{6,7},{7,6},{8,9},{9,8},{10,11... | collective-permute-start | bytes 294920 | tf_op jit(solution)/shard_map/ppermute | solution.py:25
  35.2 3.6 %copy-start.12 = (f32[8,2,768]{2,1,0:T(2,128)S(1)}, f32[8,2,768]{2,1,0:T(2,128)}, u32[]{:S(2)}) copy-start(f32[8,2,768]{2,1,0:T(2,128)} %mul.320) | copy-start | bytes 147460
  36.9 7.8 %copy-start.4 = (f32[64,768]{1,0:T(8,128)S(1)}, f32[64,768]{1,0:T(8,128)}, u32[]{:S(2)}) copy-start(f32[64,768]{1,0:T(8,128)} %get-tuple-element.71) | copy-start | bytes 589828
  43.3 32.0 %copy-start.19 = (pred[2,384]{1,0:T(4,128)(4,1)}, pred[2,384]{1,0:T(4,128)(4,1)S(1)}, u32[]{:S(2)}) copy-start(pred[2,384]{1,0:T(4,128)(4,1)S(1)} %or_and_fusion.8) | copy-start | bytes 2308
  43.8 2.2 collective-permute-start.18
  45.7 6.3 %copy-start.13 = (bf16[128,1,768]{2,0,1:T(8,128)(2,1)S(1)}, bf16[128,1,768]{2,0,1:T(8,128)(2,1)}, u32[]{:S(2)}) copy-start(bf16[128,1,768]{2,0,1:T(8,128)(2,1)} %copy.438) | copy-start | bytes 589828
  46.1 5.9 %collective-permute-start.3 = (bf16[64,768]{1,0:T(8,128)(2,1)S(1)}, bf16[64,768]{1,0:T(8,128)(2,1)S(1)}, u32[]{:S(2)}, u32[]{:S(2)}) collective-permute-start(bf16[64,768]{1,0:T(8,128)(2,1)S(1)} %get-tuple-element.58), channel_id=1, source_target_pairs={{0,2},{1,3},{2,0},{3,1},{4,6},{5,7},{6,4},{7,5},{8,10},{9,11},{10,... | collective-permute-start | bytes 294920 | tf_op jit(solution)/shard_map/ppermute | solution.py:25
  52.0 36.7 %collective-permute-start.14 = (bf16[128,768]{1,0:T(8,128)(2,1)S(1)}, bf16[128,768]{1,0:T(8,128)(2,1)}, u32[]{:S(2)}, u32[]{:S(2)}) collective-permute-start(bf16[128,768]{1,0:T(8,128)(2,1)S(1)} %bitcast.377), channel_id=1, source_target_pairs={{0,1},{1,2},{2,3},{3,4},{4,5},{5,6},{6,7},{7,8},{8,9},{9,10},{10,1... | collective-permute-start | bytes 589832 | tf_op jit(solution)/shard_map/ppermute | solution.py:19
  55.8 79.3 %collective-permute-start.15 = (f32[128,768]{1,0:T(8,128)}, f32[128,768]{1,0:T(8,128)}, u32[]{:S(2)}, u32[]{:S(2)}) collective-permute-start(f32[128,768]{1,0:T(8,128)} %bitcast.331), channel_id=1, source_target_pairs={{1,0},{2,1},{3,2},{4,3},{5,4},{6,5},{7,6},{8,7},{9,8},{10,9},{11,1... | collective-permute-start | bytes 1179656 | tf_op jit(solution)/shard_map/ppermute | solution.py:19
  57.2 11.8 %collective-permute-start.19 = (bf16[64,768]{1,0:T(8,128)(2,1)}, bf16[64,768]{1,0:T(8,128)(2,1)}, u32[]{:S(2)}, u32[]{:S(2)}) collective-permute-start(bf16[64,768]{1,0:T(8,128)(2,1)} %bitcast.336), channel_id=1, source_target_pairs={{0,2},{1,3},{2,0},{3,1},{4,6},{5,7},{6,4},{7,5},{8,10},{9,11},{10,... | collective-permute-start | bytes 294920 | tf_op jit(solution)/shard_map/ppermute | solution.py:25
  63.3 9.6 %copy-start.9 = (bf16[2,128,12,64]{1,0,3,2:T(2,128)(2,1)S(1)}, bf16[2,128,12,64]{1,0,3,2:T(2,128)(2,1)}, u32[]{:S(2)}) copy-start(bf16[2,128,12,64]{1,0,3,2:T(2,128)(2,1)} %squeeze.18) | copy-start | bytes 1179652
  63.3 9.6 %copy-start.10 = (bf16[2,128,12,64]{1,3,2,0:T(8,128)(2,1)S(1)}, bf16[2,128,12,64]{1,3,2,0:T(8,128)(2,1)}, u32[]{:S(2)}) copy-start(bf16[2,128,12,64]{1,3,2,0:T(8,128)(2,1)} %copy.257) | copy-start | bytes 1179652
  69.0 22.1 %collective-permute-start.30 = (bf16[128,768]{1,0:T(8,128)(2,1)}, bf16[128,768]{1,0:T(8,128)(2,1)S(1)}, u32[]{:S(2)}, u32[]{:S(2)}) collective-permute-start(bf16[128,768]{1,0:T(8,128)(2,1)} %bitcast.378), channel_id=1, source_target_pairs={{0,1},{1,2},{2,3},{3,4},{4,5},{5,6},{6,7},{7,8},{8,9},{9,10},{10,1... | collective-permute-start | bytes 589832 | tf_op jit(solution)/shard_map/ppermute | solution.py:19
  75.3 2.2 copy-start.2
  75.3 2.1 copy-start.15
  77.7 89.7 %collective-permute-start.31 = (f32[128,768]{1,0:T(8,128)}, f32[128,768]{1,0:T(8,128)}, u32[]{:S(2)}, u32[]{:S(2)}) collective-permute-start(f32[128,768]{1,0:T(8,128)} %bitcast.330), channel_id=1, source_target_pairs={{1,0},{2,1},{3,2},{4,3},{5,4},{6,5},{7,6},{8,7},{9,8},{10,9},{11,1... | collective-permute-start | bytes 1179656 | tf_op jit(solution)/shard_map/ppermute | solution.py:19
  79.0 17.4 %collective-permute-start.4 = (bf16[64,768]{1,0:T(8,128)(2,1)}, bf16[64,768]{1,0:T(8,128)(2,1)S(1)}, u32[]{:S(2)}, u32[]{:S(2)}) collective-permute-start(bf16[64,768]{1,0:T(8,128)(2,1)} %get-tuple-element.52), channel_id=1, source_target_pairs={{0,4},{1,5},{2,6},{3,7},{4,0},{5,1},{6,2},{7,3},{8,12},{9,13},{10,... | collective-permute-start | bytes 294920 | tf_op jit(solution)/shard_map/ppermute | solution.py:25
  88.7 16.5 %collective-permute-start.13 = (bf16[128,768]{1,0:T(8,128)(2,1)}, bf16[128,768]{1,0:T(8,128)(2,1)S(1)}, u32[]{:S(2)}, u32[]{:S(2)}) collective-permute-start(bf16[128,768]{1,0:T(8,128)(2,1)} %get-tuple-element.68), channel_id=1, source_target_pairs={{2,0},{3,1},{4,2},{5,3},{6,4},{7,5},{8,6},{9,7},{10,8},{11,9},{12,... | collective-permute-start | bytes 589832 | tf_op jit(solution)/shard_map/ppermute | solution.py:19
  91.1 19.8 %collective-permute-start.12 = (bf16[128,768]{1,0:T(8,128)(2,1)}, bf16[128,768]{1,0:T(8,128)(2,1)}, u32[]{:S(2)}, u32[]{:S(2)}) collective-permute-start(bf16[128,768]{1,0:T(8,128)(2,1)} %get-tuple-element.68), channel_id=1, source_target_pairs={{0,2},{1,3},{2,4},{3,5},{4,6},{5,7},{6,8},{7,9},{8,10},{9,11},{10,... | collective-permute-start | bytes 589832 | tf_op jit(solution)/shard_map/ppermute | solution.py:19
  96.4 5.6 %collective-permute-start.20 = (bf16[64,768]{1,0:T(8,128)(2,1)S(1)}, bf16[64,768]{1,0:T(8,128)(2,1)}, u32[]{:S(2)}, u32[]{:S(2)}) collective-permute-start(bf16[64,768]{1,0:T(8,128)(2,1)S(1)} %bitcast.383), channel_id=1, source_target_pairs={{0,4},{1,5},{2,6},{3,7},{4,0},{5,1},{6,2},{7,3},{8,12},{9,13},{10,... | collective-permute-start | bytes 294920 | tf_op jit(solution)/shard_map/ppermute | solution.py:25
  97.3 16.7 %copy-start.5 = (f32[64,12,64]{2,1,0:T(8,128)S(1)}, f32[64,12,64]{2,1,0:T(8,128)}, u32[]{:S(2)}) copy-start(f32[64,12,64]{2,1,0:T(8,128)} %mul.345) | copy-start | bytes 589828
  97.3 16.7 %copy-start.18 = (pred[64,256]{1,0:T(8,128)(4,1)S(1)}, pred[64,256]{1,0:T(8,128)(4,1)}, u32[]{:S(2)}) copy-start(pred[64,256]{1,0:T(8,128)(4,1)} %add_bitcast_fusion.1) | copy-start | bytes 49156
  102.0 14.5 %collective-permute-start.29 = (bf16[128,768]{1,0:T(8,128)(2,1)}, bf16[128,768]{1,0:T(8,128)(2,1)}, u32[]{:S(2)}, u32[]{:S(2)}) collective-permute-start(bf16[128,768]{1,0:T(8,128)(2,1)} %get-tuple-element.62), channel_id=1, source_target_pairs={{2,0},{3,1},{4,2},{5,3},{6,4},{7,5},{8,6},{9,7},{10,8},{11,9},{12,... | collective-permute-start | bytes 589832 | tf_op jit(solution)/shard_map/ppermute | solution.py:19
  105.2 18.3 %collective-permute-start.28 = (bf16[128,768]{1,0:T(8,128)(2,1)}, bf16[128,768]{1,0:T(8,128)(2,1)}, u32[]{:S(2)}, u32[]{:S(2)}) collective-permute-start(bf16[128,768]{1,0:T(8,128)(2,1)} %get-tuple-element.62), channel_id=1, source_target_pairs={{0,2},{1,3},{2,4},{3,5},{4,6},{5,7},{6,8},{7,9},{8,10},{9,11},{10,... | collective-permute-start | bytes 589832 | tf_op jit(solution)/shard_map/ppermute | solution.py:19
  110.9 17.2 %collective-permute-start.11 = (bf16[128,768]{1,0:T(8,128)(2,1)}, bf16[128,768]{1,0:T(8,128)(2,1)}, u32[]{:S(2)}, u32[]{:S(2)}) collective-permute-start(bf16[128,768]{1,0:T(8,128)(2,1)} %get-tuple-element.56), channel_id=1, source_target_pairs={{4,0},{5,1},{6,2},{7,3},{8,4},{9,5},{10,6},{11,7},{12,8},{13,9},{1... | collective-permute-start | bytes 589832 | tf_op jit(solution)/shard_map/ppermute | solution.py:19
  116.5 25.0 %collective-permute-start.10 = (bf16[128,768]{1,0:T(8,128)(2,1)}, bf16[128,768]{1,0:T(8,128)(2,1)}, u32[]{:S(2)}, u32[]{:S(2)}) collective-permute-start(bf16[128,768]{1,0:T(8,128)(2,1)} %get-tuple-element.56), channel_id=1, source_target_pairs={{0,4},{1,5},{2,6},{3,7},{4,8},{5,9},{6,10},{7,11},{8,12},{9,13},{1... | collective-permute-start | bytes 589832 | tf_op jit(solution)/shard_map/ppermute | solution.py:19
  123.4 33.7 %collective-permute-start.27 = (bf16[128,768]{1,0:T(8,128)(2,1)}, bf16[128,768]{1,0:T(8,128)(2,1)}, u32[]{:S(2)}, u32[]{:S(2)}) collective-permute-start(bf16[128,768]{1,0:T(8,128)(2,1)} %get-tuple-element.60), channel_id=1, source_target_pairs={{4,0},{5,1},{6,2},{7,3},{8,4},{9,5},{10,6},{11,7},{12,8},{13,9},{1... | collective-permute-start | bytes 589832 | tf_op jit(solution)/shard_map/ppermute | solution.py:19
  128.1 32.0 %collective-permute-start.26 = (bf16[128,768]{1,0:T(8,128)(2,1)}, bf16[128,768]{1,0:T(8,128)(2,1)}, u32[]{:S(2)}, u32[]{:S(2)}) collective-permute-start(bf16[128,768]{1,0:T(8,128)(2,1)} %get-tuple-element.60), channel_id=1, source_target_pairs={{0,4},{1,5},{2,6},{3,7},{4,8},{5,9},{6,10},{7,11},{8,12},{9,13},{1... | collective-permute-start | bytes 589832 | tf_op jit(solution)/shard_map/ppermute | solution.py:19
  135.2 11.2 %collective-permute-start.5 = (bf16[64,768]{1,0:T(8,128)(2,1)}, bf16[64,768]{1,0:T(8,128)(2,1)}, u32[]{:S(2)}, u32[]{:S(2)}) collective-permute-start(bf16[64,768]{1,0:T(8,128)(2,1)} %fusion.95), channel_id=1, source_target_pairs={{0,8},{1,9},{2,10},{3,11},{4,12},{5,13},{6,14},{7,15},{8,0},{9,1},... | collective-permute-start | bytes 294920 | tf_op jit(solution)/shard_map/ppermute | solution.py:25
  141.4 15.0 %copy-start.11 = (bf16[64,1,768]{2,0,1:T(8,128)(2,1)S(1)}, bf16[64,1,768]{2,0,1:T(8,128)(2,1)}, u32[]{:S(2)}) copy-start(bf16[64,1,768]{2,0,1:T(8,128)(2,1)} %copy.437) | copy-start | bytes 294916
  141.5 29.7 %collective-permute-start.9 = (bf16[128,768]{1,0:T(8,128)(2,1)}, bf16[128,768]{1,0:T(8,128)(2,1)}, u32[]{:S(2)}, u32[]{:S(2)}) collective-permute-start(bf16[128,768]{1,0:T(8,128)(2,1)} %get-tuple-element.50), channel_id=1, source_target_pairs={{8,0},{9,1},{10,2},{11,3},{12,4},{13,5},{14,6},{15,7},{16,8},{17,9... | collective-permute-start | bytes 589832 | tf_op jit(solution)/shard_map/ppermute | solution.py:19
  145.5 21.9 %copy-start.14 = (f32[12,32]{1,0:T(8,128)}, f32[12,32]{1,0:T(8,128)S(1)}, u32[]{:S(2)}) copy-start(f32[12,32]{1,0:T(8,128)S(1)} %get-tuple-element.104) | copy-start | bytes 4612
  146.3 5.4 %collective-permute-start.21 = (bf16[64,768]{1,0:T(8,128)(2,1)}, bf16[64,768]{1,0:T(8,128)(2,1)S(1)}, u32[]{:S(2)}, u32[]{:S(2)}) collective-permute-start(bf16[64,768]{1,0:T(8,128)(2,1)} %bitcast.361), channel_id=1, source_target_pairs={{0,8},{1,9},{2,10},{3,11},{4,12},{5,13},{6,14},{7,15},{8,0},{9,1},... | collective-permute-start | bytes 294920 | tf_op jit(solution)/shard_map/ppermute | solution.py:25
  151.8 27.7 %collective-permute-start.8 = (bf16[128,768]{1,0:T(8,128)(2,1)}, bf16[128,768]{1,0:T(8,128)(2,1)}, u32[]{:S(2)}, u32[]{:S(2)}) collective-permute-start(bf16[128,768]{1,0:T(8,128)(2,1)} %get-tuple-element.50), channel_id=1, source_target_pairs={{0,8},{1,9},{2,10},{3,11},{4,12},{5,13},{6,14},{7,15},{8,16},{9,17... | collective-permute-start | bytes 589832 | tf_op jit(solution)/shard_map/ppermute | solution.py:19
  157.1 28.1 %collective-permute-start.25 = (bf16[128,768]{1,0:T(8,128)(2,1)}, bf16[128,768]{1,0:T(8,128)(2,1)}, u32[]{:S(2)}, u32[]{:S(2)}) collective-permute-start(bf16[128,768]{1,0:T(8,128)(2,1)} %get-tuple-element.54), channel_id=1, source_target_pairs={{8,0},{9,1},{10,2},{11,3},{12,4},{13,5},{14,6},{15,7},{16,8},{17,9... | collective-permute-start | bytes 589832 | tf_op jit(solution)/shard_map/ppermute | solution.py:19
  160.1 33.6 %collective-permute-start.24 = (bf16[128,768]{1,0:T(8,128)(2,1)}, bf16[128,768]{1,0:T(8,128)(2,1)}, u32[]{:S(2)}, u32[]{:S(2)}) collective-permute-start(bf16[128,768]{1,0:T(8,128)(2,1)} %get-tuple-element.54), channel_id=1, source_target_pairs={{0,8},{1,9},{2,10},{3,11},{4,12},{5,13},{6,14},{7,15},{8,16},{9,17... | collective-permute-start | bytes 589832 | tf_op jit(solution)/shard_map/ppermute | solution.py:19
  167.4 29.8 %collective-permute-start.7 = (bf16[128,768]{1,0:T(8,128)(2,1)}, bf16[128,768]{1,0:T(8,128)(2,1)}, u32[]{:S(2)}, u32[]{:S(2)}) collective-permute-start(bf16[128,768]{1,0:T(8,128)(2,1)} %fusion.67), channel_id=1, source_target_pairs={{16,0},{17,1},{18,2},{19,3},{20,4},{21,5},{22,6},{23,7},{24,8},{25... | collective-permute-start | bytes 589832 | tf_op jit(solution)/shard_map/ppermute | solution.py:19
  171.2 27.8 %collective-permute-start.6 = (bf16[128,768]{1,0:T(8,128)(2,1)}, bf16[128,768]{1,0:T(8,128)(2,1)}, u32[]{:S(2)}, u32[]{:S(2)}) collective-permute-start(bf16[128,768]{1,0:T(8,128)(2,1)} %fusion.67), channel_id=1, source_target_pairs={{0,16},{1,17},{2,18},{3,19},{4,20},{5,21},{6,22},{7,23},{8,24},{9,... | collective-permute-start | bytes 589832 | tf_op jit(solution)/shard_map/ppermute | solution.py:19
  179.5 73.0 %collective-permute-start.23 = (bf16[128,768]{1,0:T(8,128)(2,1)}, bf16[128,768]{1,0:T(8,128)(2,1)}, u32[]{:S(2)}, u32[]{:S(2)}) collective-permute-start(bf16[128,768]{1,0:T(8,128)(2,1)} %fusion.76), channel_id=1, source_target_pairs={{16,0},{17,1},{18,2},{19,3},{20,4},{21,5},{22,6},{23,7},{24,8},{25... | collective-permute-start | bytes 589832 | tf_op jit(solution)/shard_map/ppermute | solution.py:19
  185.2 69.1 %collective-permute-start.22 = (bf16[128,768]{1,0:T(8,128)(2,1)}, bf16[128,768]{1,0:T(8,128)(2,1)}, u32[]{:S(2)}, u32[]{:S(2)}) collective-permute-start(bf16[128,768]{1,0:T(8,128)(2,1)} %fusion.76), channel_id=1, source_target_pairs={{0,16},{1,17},{2,18},{3,19},{4,20},{5,21},{6,22},{7,23},{8,24},{9,... | collective-permute-start | bytes 589832 | tf_op jit(solution)/shard_map/ppermute | solution.py:19
  264.7 1.7 copy-start.17
  271.1 1.1 copy-start.16
  271.1 1.8 copy-start.6
  271.1 1.8 copy-start.7
  271.1 1.8 copy-start.8
where the time goes:
time: 281 us; the launch traced here: 278 us
  local copies, waits for them, and re-layouts  106 us (38%)
  starting transfers between devices  91.1 us (32%)
  other arithmetic  40.1 us (14%)
  matrix products  27.8 us (10%)
  waiting for transfers between devices  11.9 us (4%)
    ppermute x24, starting transfers between devices, passed_along(): return lax.ppermute(block, axis, route)  72.5 us
    ppermute x18, local copies, waits for them, and re-layouts, passed_along(): return lax.ppermute(block, axis, route)  28.7 us
    ppermute x8, starting transfers between devices, from_partner(): return lax.ppermute(value, axis, pairs)  18.6 us
    reshape x10, local copies, waits for them, and re-layouts, widen(): return tuple((jnp.repeat(part, 2, axis=0) for part in combined))  12.6 us
    ppermute x8, waiting for transfers between devices, from_partner(): return lax.ppermute(value, axis, pairs)  11.9 us
    broadcast_in_dim x12, local copies, waits for them, and re-layouts, widen(): return tuple((jnp.repeat(part, 2, axis=0) for part in combined))  11.2 us
    dot_general x5, matrix products, coarse_terms(): jnp.einsum('bqhe,bkhe->bhqk', query_heads, key_heads, precision=HIGHEST)  11 us
    dot_general x5, matrix products, coarse_terms(): jnp.einsum('bhqk,bkhe->bqhe', weights, value_heads, precision=HIGHEST)  10.8 us
  transfers between devices with their start and end apart: 32, of which 4 were waited for; matrix products, arithmetic and copies ran while one was open for 53% of the time, Pallas kernels for 0%

commit v1 on v0

v1 whole, which is shorter than its diff:
```python
import functools
import math

import jax
import jax.numpy as jnp
from jax import lax
from jax.experimental import pallas as pl
from jax.experimental.pallas import tpu as pltpu
from jax.sharding import PartitionSpec as P

HEADS = 12
BLOCK = 128
LANES = 128
LOG_TWO = math.log(2.0)
NEVER = -1e30
MESH = pl.DeviceIdType.MESH


class Plan:
    def __init__(self, length, features, outer, inner):
        self.length, self.features = length, features
        self.inner = inner
        self.devices = outer * inner
        self.chips = self.devices // 2
        self.top = self.devices.bit_length() - 1
        self.levels = list(range(1, self.top + 1))
        self.deep = list(range(2, self.top + 1))
        self.rows = {l: length >> l for l in self.levels}
        self.padded = {l: max(8, length >> l) for l in self.levels}
        self.offset, total = {}, 0
        for l in self.levels:
            self.offset[l] = total
            total += self.padded[l]
        self.pooled_rows = total
        self.pairs = features // LANES

    def link_type(self, l):
        return jnp.bfloat16 if self.padded[l] >= 16 else jnp.float32

    def half_chips(self, l):
        return 2**l // 8

    def blocks(self, l):
        return self.devices // 2 ** (l - 1)


def pool_matrix(rows, columns, step):
    r = lax.broadcasted_iota(jnp.int32, (rows, columns), 0)
    c = lax.broadcasted_iota(jnp.int32, (rows, columns), 1)
    return jnp.where(c // step == r, 1.0 / step, 0.0).astype(jnp.float32)


def attend(q, keys, values, bias):
    n = q.shape[0]
    w = keys.shape[0]
    first = lax.broadcasted_iota(jnp.int32, (n, LANES), 1) < LANES // 2
    zero = jnp.zeros_like(q)
    both = jnp.concatenate([jnp.where(first, q, zero), jnp.where(first, zero, q)], axis=0)
    s = lax.dot_general(
        both.astype(jnp.bfloat16), keys, (((1,), (1,)), ((), ())), preferred_element_type=jnp.float32
    )
    if bias is not None:
        if bias.shape[0] == n:
            bias = jnp.concatenate([bias, bias], axis=0)
        s = s + bias
    m = jnp.max(s, axis=1, keepdims=True)
    p = jnp.exp(s - m).astype(jnp.bfloat16)
    right = jnp.concatenate([values, jnp.ones((w, LANES), jnp.bfloat16)], axis=1)
    r = jnp.dot(p, right, preferred_element_type=jnp.float32)
    o = jnp.where(first, r[:n, :LANES], r[n:, :LANES])
    z = jnp.where(first, r[:n, LANES:], r[n:, LANES:])
    wide = jnp.where(
        first, jnp.broadcast_to(m[:n], (n, LANES)), jnp.broadcast_to(m[n:], (n, LANES))
    )
    return wide, z, o


def merge(one, two):
    top = jnp.maximum(one[0], two[0])
    a = jnp.exp(one[0] - top)
    b = jnp.exp(two[0] - top)
    return top, a * one[1] + b * two[1], a * one[2] + b * two[2]


def kernel(plan, names, *refs):
    R = dict(zip(names, refs))
    q_ref, k_ref, v_ref, out_ref = R["q"], R["k"], R["v"], R["out"]
    feats, length = plan.features, plan.length
    half = BLOCK // 2
    pos = lax.axis_index("seqa") * plan.inner + lax.axis_index("seqb")
    core = lax.rem(pos, 2)
    other = 1 - core
    chip = lax.div(pos, 2)
    has_left = pos > 0
    has_right = pos < plan.devices - 1

    def device(p):
        return (lax.div(p, plan.inner), lax.rem(p, plan.inner))

    sibling = device(2 * chip + other)

    barrier = pltpu.get_barrier_semaphore()

    def greet(i, carry):
        @pl.when(i != chip)
        def _():
            pl.semaphore_signal(barrier, inc=1, device_id=device(2 * i + core), device_id_type=MESH)

        return carry

    lax.fori_loop(0, plan.chips, greet, 0)
    pl.semaphore_signal(barrier, inc=1, device_id=sibling, device_id_type=MESH)
    far = jnp.where(core == 0, pos - 1, pos + 1)
    has_far = (far >= 0) & (far < plan.devices)

    @pl.when(has_far)
    def _():
        pl.semaphore_signal(barrier, inc=1, device_id=device(far), device_id_type=MESH)

    pool = jnp.concatenate(
        [pool_matrix(plan.padded[l], length, 2**l) for l in plan.levels], axis=0
    ).astype(jnp.bfloat16)
    R["qp"][...] = jnp.dot(pool, q_ref[...], preferred_element_type=jnp.float32) * 0.125
    for ref, at in ((k_ref, 0), (v_ref, feats)):
        pooled = jnp.dot(pool, ref[...], preferred_element_type=jnp.float32)
        for l in plan.levels:
            part = pooled[plan.offset[l] : plan.offset[l] + plan.padded[l]]
            send = R[f"send{l}"]
            send[:, at : at + feats] = part.astype(send.dtype)

    facts = {}
    for l in plan.deep:
        span = 2 ** (l - 1)
        J = lax.div(pos, span)
        b = jnp.where(lax.rem(pos, span) >= span // 2, 1, 0)
        left_ok = J > 0
        right_ok = J < plan.blocks(l) - 1
        mid_ok = jnp.where(b == 1, J, plan.blocks(l) - 1 - J) > 0
        facts[l] = (J, b, left_ok, right_ok, (left_ok, mid_ok, right_ok))
        buf = R[f"buf{l}"]
        for slot in range(3):
            @pl.when(jnp.logical_not(facts[l][4][slot]))
            def _(buf=buf, slot=slot, l=l):
                if l == 2:
                    buf[slot] = jnp.zeros(buf.shape[1:], buf.dtype)
                else:
                    for c in range(2):
                        buf[c, slot] = jnp.zeros(buf.shape[2:], buf.dtype)

    near = R["near"]

    @pl.when(jnp.logical_not(has_left))
    def _():
        R["fk"][0] = jnp.zeros((BLOCK, feats), jnp.bfloat16)
        R["fv"][0] = jnp.zeros((BLOCK, feats), jnp.bfloat16)
        near[0:half] = jnp.zeros((half, 2 * feats), jnp.bfloat16)

    @pl.when(jnp.logical_not(has_right))
    def _():
        R["fk"][1] = jnp.zeros((BLOCK, feats), jnp.bfloat16)
        R["fv"][1] = jnp.zeros((BLOCK, feats), jnp.bfloat16)
        near[3 * half :] = jnp.zeros((half, 2 * feats), jnp.bfloat16)

    pl.semaphore_wait(barrier, plan.chips + jnp.where(has_far, 1, 0))

    def remote(src, dst, send_sem, recv_sem, target):
        return pltpu.make_async_remote_copy(
            src_ref=src, dst_ref=dst, send_sem=send_sem, recv_sem=recv_sem,
            device_id=target, device_id_type=MESH,
        )

    def deep_copies(l, t, act):
        J, b, left_ok, right_ok, _ = facts[l]
        send, buf = R[f"send{l}"], R[f"buf{l}"]
        ss, rs = R[f"ss{l}"], R[f"rs{l}"]
        if l == 2:
            group, mine, a = 1, 0, core
            ok_r = right_ok
            ok_l = left_ok
        else:
            m = plan.half_chips(l)
            group = 2 * m
            mine = lax.rem(chip, m)
            a = jnp.where(t >= m, 1, 0)
            ok_r = right_ok & (a >= b)
            ok_l = left_ok & (a <= b)
        for side, ok, step in ((0, ok_r, 1), (1, ok_l, -1)):
            slot = b + side
            dst = buf.at[slot] if l == 2 else buf.at[core, slot, mine]

            @pl.when(ok)
            def _(side=side, step=step, slot=slot, dst=dst):
                target = device(2 * ((J + step) * group + t) + core)
                act(remote(send, dst, ss.at[side, t], rs.at[slot], target))

    def all_deep(act):
        for l in reversed(plan.deep):
            if l == 2:
                deep_copies(l, 0, act)
            else:
                def body(t, carry, l=l):
                    deep_copies(l, t, act)
                    return carry

                lax.fori_loop(0, 2 * plan.half_chips(l), body, 0)

    all_deep(lambda copy: copy.start())

    def neighbour_copies(act):
        send1 = R["send1"]
        fs, fr = R["fs"], R["fr"]

        @pl.when(has_right)
        def _():
            t = device(pos + 1)
            act(remote(k_ref.at[pl.ds(BLOCK, BLOCK)], R["fk"].at[0], fs.at[0], fr.at[0], t))
            act(remote(v_ref.at[pl.ds(BLOCK, BLOCK)], R["fv"].at[0], fs.at[1], fr.at[1], t))
            act(remote(send1.at[pl.ds(0, half)], near.at[pl.ds(0, half)], fs.at[2], fr.at[2], t))

        @pl.when(has_left)
        def _():
            t = device(pos - 1)
            act(remote(k_ref.at[pl.ds(0, BLOCK)], R["fk"].at[1], fs.at[3], fr.at[3], t))
            act(remote(v_ref.at[pl.ds(0, BLOCK)], R["fv"].at[1], fs.at[4], fr.at[4], t))
            act(remote(send1.at[pl.ds(half, half)], near.at[pl.ds(3 * half, half)], fs.at[5], fr.at[5], t))

    neighbour_copies(lambda copy: copy.start())

    def lanes(hp, base=0):
        return pl.ds(pl.multiple_of(base + hp * LANES, LANES), LANES)

    def own(hp, carry):
        ls = lanes(hp)
        q = q_ref[:, ls].astype(jnp.float32) * 0.125
        m, z, o = attend(q, k_ref[:, ls], v_ref[:, ls], None)
        R["fine"][0, :, ls] = m
        R["fine"][1, :, ls] = z
        R["fine"][2, :, ls] = o
        return carry

    lax.fori_loop(0, plan.pairs, own, 0, unroll=2)

    def arrived(ref, sem):
        pltpu.make_async_copy(ref, ref, sem).wait()

    def relay(l, slot):
        buf = R[f"buf{l}"]
        if l == 2:
            return remote(buf.at[slot], buf.at[slot], R["ys2"].at[slot], R["yr2"].at[slot], sibling)
        return remote(
            buf.at[core, slot], buf.at[core, slot], R[f"ys{l}"].at[slot], R[f"yr{l}"].at[slot], sibling
        )

    for l in reversed(plan.deep):
        buf = R[f"buf{l}"]
        for slot in range(3):
            ok = facts[l][4][slot]
            if l == 2:
                direct = {0: core == 0, 1: core >= 0, 2: core == 1}[slot]

                @pl.when(ok & direct)
                def _(l=l, slot=slot, buf=buf):
                    arrived(buf.at[slot], R[f"rs{l}"].at[slot])
                    if slot != 1:
                        relay(l, slot).start()
            else:
                @pl.when(ok)
                def _(l=l, slot=slot, buf=buf):
                    arrived(buf.at[core, slot], R[f"rs{l}"].at[slot])
                    relay(l, slot).start()

    @pl.when(has_left)
    def _():
        arrived(R["fk"].at[0], R["fr"].at[0])
        arrived(R["fv"].at[0], R["fr"].at[1])
        arrived(near.at[pl.ds(0, half)], R["fr"].at[2])

    @pl.when(has_right)
    def _():
        arrived(R["fk"].at[1], R["fr"].at[3])
        arrived(R["fv"].at[1], R["fr"].at[4])
        arrived(near.at[pl.ds(3 * half, half)], R["fr"].at[5])

    pool1 = pool_matrix(half, BLOCK, 2).astype(jnp.bfloat16)
    for side in range(2):
        for name, at in (("fk", 0), ("fv", feats)):
            part = jnp.dot(pool1, R[name][side], preferred_element_type=jnp.float32)
            near[half * (1 + side) : half * (2 + side), at : at + feats] = part.astype(jnp.bfloat16)

    gone_left = jnp.where(has_left, 0.0, NEVER).astype(jnp.float32)
    gone_right = jnp.where(has_right, 0.0, NEVER).astype(jnp.float32)
    row = lax.broadcasted_iota(jnp.int32, (BLOCK, 2 * BLOCK), 0)
    col = lax.broadcasted_iota(jnp.int32, (BLOCK, 2 * BLOCK), 1)
    upper = row >= half
    quarter = col // half
    hidden = (upper & (quarter == 2)) | (jnp.logical_not(upper) & (quarter == 1))
    R["bias"][...] = jnp.where(hidden, NEVER, 0.0) + jnp.where(quarter < 2, gone_left, gone_right)

    def beside(hp, carry):
        ls = lanes(hp)
        vs = lanes(hp, feats)
        fine = R["fine"]
        for side, gone in ((0, gone_left), (1, gone_right)):
            rows = slice(side * BLOCK, (side + 1) * BLOCK)
            q = q_ref[rows, ls].astype(jnp.float32) * 0.125
            m, z, o = attend(q, R["fk"][side, :, ls], R["fv"][side, :, ls], None)
            m = m + gone
            both = merge((m, z, o), (fine[0, rows, ls], fine[1, rows, ls], fine[2, rows, ls]))
            for i in range(3):
                fine[i, rows, ls] = both[i]
        m, z, o = attend(R["qp"][0:BLOCK, ls], near[:, ls], near[:, vs], R["bias"][...])
        R["first"][0, :, ls] = m + LOG_TWO
        R["first"][1, :, ls] = z
        R["first"][2, :, ls] = o
        return carry

    lax.fori_loop(0, plan.pairs, beside, 0, unroll=2)

    for l in reversed(plan.deep):
        buf = R[f"buf{l}"]
        for slot in range(3):
            ok = facts[l][4][slot]
            if l == 2:
                if slot == 1:
                    continue

                @pl.when(ok & (core == (1 if slot == 0 else 0)))
                def _(slot=slot, buf=buf):
                    arrived(buf.at[slot], R["yr2"].at[slot])
            else:
                @pl.when(ok)
                def _(l=l, slot=slot, buf=buf):
                    arrived(buf.at[other, slot], R[f"yr{l}"].at[slot])

    def deep_bias(l):
        slots = R[f"buf{l}"].shape[:-1]
        width = math.prod(slots)
        per_slot = plan.padded[l] * (1 if l == 2 else plan.half_chips(l))
        c = lax.broadcasted_iota(jnp.int32, (1, width), 1)
        slot = lax.rem(c // per_slot, 3)
        gone = [jnp.where(ok, 0.0, NEVER).astype(jnp.float32) for ok in facts[l][4]]
        bias = jnp.where(slot == 0, gone[0], jnp.where(slot == 1, gone[1], gone[2]))
        if plan.rows[l] < plan.padded[l]:
            bias = jnp.where(lax.rem(c, plan.padded[l]) < plan.rows[l], bias, NEVER)
        return bias

    def deepest(hp, carry):
        ls = lanes(hp)
        vs = lanes(hp, feats)

        def widen(l, terms):
            wide = R[f"wide{l}"]
            n = terms[0].shape[0]
            for i in range(3):
                view = wide.at[hp, i]
                view[pl.ds(0, n, stride=2), :] = terms[i]
                view[pl.ds(1, n, stride=2), :] = terms[i]
            keep = length if l == 1 else plan.padded[l - 1]
            return tuple(wide[hp, i][:keep] for i in range(3))

        current = None
        for l in reversed(plan.levels):
            if l == 1:
                terms = tuple(R["first"][i, :, ls] for i in range(3))
            else:
                buf = R[f"buf{l}"]
                width = math.prod(buf.shape[:-1])
                at = (slice(None),) * (len(buf.shape) - 1)
                keys = buf[at + (ls,)].reshape(width, LANES).astype(jnp.bfloat16)
                values = buf[at + (vs,)].reshape(width, LANES).astype(jnp.bfloat16)
                q = R["qp"][plan.offset[l] : plan.offset[l] + plan.padded[l], ls]
                m, z, o = attend(q, keys, values, deep_bias(l))
                terms = (m + l * LOG_TWO, z, o)
            current = terms if current is None else merge(current, terms)
            current = widen(l, current)
        fine = tuple(R["fine"][i, :, ls] for i in range(3))
        _, z, o = merge(current, fine)
        out_ref[:, ls] = (o / z).astype(jnp.bfloat16)
        return carry

    lax.fori_loop(0, plan.pairs, deepest, 0, unroll=2)

    all_deep(lambda copy: copy.wait_send())
    neighbour_copies(lambda copy: copy.wait_send())
    for l in plan.deep:
        for slot in range(3):
            ok = facts[l][4][slot]
            if l == 2:
                if slot == 1:
                    continue
                ok = ok & (core == (0 if slot == 0 else 1))

            @pl.when(ok)
            def _(l=l, slot=slot):
                relay(l, slot).wait_send()


def shards(plan, q, k, v):
    f, length = plan.features, plan.length
    scratch = {}
    scratch["qp"] = pltpu.VMEM((plan.pooled_rows, f), jnp.float32)
    for l in plan.levels:
        kind = plan.link_type(l)
        scratch[f"send{l}"] = pltpu.VMEM((plan.padded[l], 2 * f), kind)
        if l == 1:
            continue
        sem = pltpu.SemaphoreType.DMA
        if l == 2:
            scratch["buf2"] = pltpu.VMEM((3, plan.padded[2], 2 * f), kind)
            scratch["ss2"] = sem((2, 1))
        else:
            m = plan.half_chips(l)
            scratch[f"buf{l}"] = pltpu.VMEM((2, 3, m, plan.padded[l], 2 * f), kind)
            scratch[f"ss{l}"] = sem((2, 2 * m))
        scratch[f"rs{l}"] = sem((3,))
        scratch[f"ys{l}"] = sem((3,))
        scratch[f"yr{l}"] = sem((3,))
    scratch["fk"] = pltpu.VMEM((2, BLOCK, f), jnp.bfloat16)
    scratch["fv"] = pltpu.VMEM((2, BLOCK, f), jnp.bfloat16)
    scratch["near"] = pltpu.VMEM((2 * BLOCK, 2 * f), jnp.bfloat16)
    scratch["fs"] = pltpu.SemaphoreType.DMA((6,))
    scratch["fr"] = pltpu.SemaphoreType.DMA((6,))
    scratch["fine"] = pltpu.VMEM((3, length, f), jnp.float32)
    scratch["first"] = pltpu.VMEM((3, BLOCK, f), jnp.float32)
    scratch["bias"] = pltpu.VMEM((BLOCK, 2 * BLOCK), jnp.float32)
    for l in plan.levels:
        scratch[f"wide{l}"] = pltpu.VMEM((plan.pairs, 3, 2 * plan.padded[l], LANES), jnp.float32)
    names = ["q", "k", "v", "out"] + list(scratch)
    return pl.pallas_call(
        functools.partial(kernel, plan, names),
        out_shape=jax.ShapeDtypeStruct((length, f), jnp.bfloat16),
        in_specs=[pl.BlockSpec(memory_space=pltpu.VMEM)] * 3,
        out_specs=pl.BlockSpec(memory_space=pltpu.VMEM),
        scratch_shapes=list(scratch.values()),
        compiler_params=pltpu.CompilerParams(
            collective_id=0, has_side_effects=True, vmem_limit_bytes=56 * 2**20
        ),
        name="hier_attention",
    )(q, k, v)


def solution(mesh):
    outer, inner = mesh.shape["seqa"], mesh.shape["seqb"]
    spec = P(("seqa", "seqb"), None)

    def part(q, k, v):
        plan = Plan(q.shape[0], q.shape[1], outer, inner)
        return shards(plan, q, k, v)

    return jax.shard_map(part, mesh=mesh, in_specs=(spec,) * 3, out_specs=spec, check_vma=False)
```

time: 281 us -> 53.3 us (0.19)
  the two profiles are of different devices: /device:TPU:0 before, /device:TPU:1 now
where the time goes in v1:
time: 53.3 us; the launch traced here: 53.1 us
  Pallas kernels  51.4 us (96%)
  local copies, waits for them, and re-layouts  1.77 us (3%)
    pallas_call x1, Pallas kernels, shards(): pl.pallas_call(functools.partial(kernel, plan, names), out_shape=jax.Shap...  51.4 us
    unnamed x1, local copies, waits for them, and re-layouts  1.77 us

profile of v1, /device:TPU:1, one launch (start us, length us, event | category | flops | bytes accessed | tf_op | source)
XLA Modules:
  0.0 53.1 jit_solution(13637220468273586418)
XLA Ops:
  0.0 51.4 %hier_attention.1 = bf16[256,768]{1,0:T(8,128)(2,1)} custom-call(bf16[256,768]{1,0:T(8,128)(2,1)} %refs_0_.1, bf16[256,768]{1,0:T(8,128)(2,1)} %refs_1_.1, bf16[256,768]{1,0:T(8,128)(2,1)} %refs_2_.1), custom_call_target="tpu_custom_call" | custom-call | tf_op jit(solution)/shard_map/hier_attention/pallas_call | solution.py:429
  51.4 1.8 %copy.5 = bf16[256,768]{1,0:T(8,128)(2,1)} copy(bf16[256,768]{1,0:T(8,128)(2,1)} %hier_attention.1) | data formatting | bytes 786432

commit v2 on v1

--- a/solution.py
+++ b/solution.py
@@ -34,8 +34,13 @@
         self.pooled_rows = total
         self.pairs = features // LANES
 
-    def link_type(self, l):
-        return jnp.bfloat16 if self.padded[l] >= 16 else jnp.float32
+    def packed(self, l):
+        return self.padded[l] < 16
+
+    def link_shape(self, l):
+        if self.packed(l):
+            return (16, self.features)
+        return (self.padded[l], 2 * self.features)
 
     def half_chips(self, l):
         return 2**l // 8
@@ -117,17 +122,6 @@
     def _():
         pl.semaphore_signal(barrier, inc=1, device_id=device(far), device_id_type=MESH)
 
-    pool = jnp.concatenate(
-        [pool_matrix(plan.padded[l], length, 2**l) for l in plan.levels], axis=0
-    ).astype(jnp.bfloat16)
-    R["qp"][...] = jnp.dot(pool, q_ref[...], preferred_element_type=jnp.float32) * 0.125
-    for ref, at in ((k_ref, 0), (v_ref, feats)):
-        pooled = jnp.dot(pool, ref[...], preferred_element_type=jnp.float32)
-        for l in plan.levels:
-            part = pooled[plan.offset[l] : plan.offset[l] + plan.padded[l]]
-            send = R[f"send{l}"]
-            send[:, at : at + feats] = part.astype(send.dtype)
-
     facts = {}
     for l in plan.deep:
         span = 2 ** (l - 1)
@@ -169,14 +163,52 @@
             device_id=target, device_id_type=MESH,
         )
 
+    def neighbour_copies(act, which):
+        send1 = R["send1"]
+        fs, fr = R["fs"], R["fr"]
+        for side, ok, step in ((0, has_right, 1), (1, has_left, -1)):
+            @pl.when(ok)
+            def _(side=side, step=step):
+                t = device(pos + step)
+                base = 3 * side
+                for i in which:
+                    if i < 2:
+                        src = (k_ref, v_ref)[i].at[pl.ds(BLOCK * (1 - side), BLOCK)]
+                        dst = R[("fk", "fv")[i]].at[side]
+                    else:
+                        src = send1.at[pl.ds(half * side, half)]
+                        dst = near.at[pl.ds(3 * half * side, half)]
+                    act(remote(src, dst, fs.at[base + i], fr.at[base + i], t))
+
+    neighbour_copies(lambda copy: copy.start(), (0, 1))
+
+    pool = jnp.concatenate(
+        [pool_matrix(plan.padded[l], length, 2**l) for l in plan.levels], axis=0
+    ).astype(jnp.bfloat16)
+    R["qp"][...] = jnp.dot(pool, q_ref[...], preferred_element_type=jnp.float32) * 0.125
+    tops = {}
+    for ref, at in ((k_ref, 0), (v_ref, feats)):
+        pooled = jnp.dot(pool, ref[...], preferred_element_type=jnp.float32)
+        for l in plan.levels:
+            part = pooled[plan.offset[l] : plan.offset[l] + plan.padded[l]]
+            send = R[f"send{l}"]
+            if plan.packed(l):
+                tops.setdefault(l, []).append(part)
+            else:
+                send[:, at : at + feats] = part.astype(jnp.bfloat16)
+    for l, parts in tops.items():
+        R[f"send{l}"][...] = jnp.concatenate(parts, axis=0).astype(jnp.bfloat16)
+
+    neighbour_copies(lambda copy: copy.start(), (2,))
+
     def deep_copies(l, t, act):
         J, b, left_ok, right_ok, _ = facts[l]
         send, buf = R[f"send{l}"], R[f"buf{l}"]
         ss, rs = R[f"ss{l}"], R[f"rs{l}"]
         if l == 2:
             group, mine, a = 1, 0, core
-            ok_r = right_ok
-            ok_l = left_ok
+            ok_r = right_ok & (core == 0)
+            ok_l = left_ok & (core == 1)
         else:
             m = plan.half_chips(l)
             group = 2 * m
@@ -206,26 +238,6 @@
 
     all_deep(lambda copy: copy.start())
 
-    def neighbour_copies(act):
-        send1 = R["send1"]
-        fs, fr = R["fs"], R["fr"]
-
-        @pl.when(has_right)
-        def _():
-            t = device(pos + 1)
-            act(remote(k_ref.at[pl.ds(BLOCK, BLOCK)], R["fk"].at[0], fs.at[0], fr.at[0], t))
-            act(remote(v_ref.at[pl.ds(BLOCK, BLOCK)], R["fv"].at[0], fs.at[1], fr.at[1], t))
-            act(remote(send1.at[pl.ds(0, half)], near.at[pl.ds(0, half)], fs.at[2], fr.at[2], t))
-
-        @pl.when(has_left)
-        def _():
-            t = device(pos - 1)
-            act(remote(k_ref.at[pl.ds(0, BLOCK)], R["fk"].at[1], fs.at[3], fr.at[3], t))
-            act(remote(v_ref.at[pl.ds(0, BLOCK)], R["fv"].at[1], fs.at[4], fr.at[4], t))
-            act(remote(send1.at[pl.ds(half, half)], near.at[pl.ds(3 * half, half)], fs.at[5], fr.at[5], t))
-
-    neighbour_copies(lambda copy: copy.start())
-
     def lanes(hp, base=0):
         return pl.ds(pl.multiple_of(base + hp * LANES, LANES), LANES)
 
@@ -245,29 +257,43 @@
 
     def relay(l, slot):
         buf = R[f"buf{l}"]
+        ys, yr = R[f"ys{l}"].at[slot], R[f"yr{l}"].at[slot]
         if l == 2:
-            return remote(buf.at[slot], buf.at[slot], R["ys2"].at[slot], R["yr2"].at[slot], sibling)
-        return remote(
-            buf.at[core, slot], buf.at[core, slot], R[f"ys{l}"].at[slot], R[f"yr{l}"].at[slot], sibling
-        )
-
-    for l in reversed(plan.deep):
+            src = R["stage"] if slot == 1 else buf.at[slot]
+            return remote(src, buf.at[slot], ys, yr, sibling)
+        return remote(buf.at[core, slot], buf.at[core, slot], ys, yr, sibling)
+
+    def relays_out(l):
+        ok = facts[l][4]
+        if l == 2:
+            return ((0, ok[0] & (core == 0)), (1, has_far), (2, ok[2] & (core == 1)))
+        return tuple((slot, ok[slot]) for slot in range(3))
+
+    def relays_in(l):
+        ok = facts[l][4]
+        if l == 2:
+            return ((0, ok[0] & (core == 1)), (1, ok[1]), (2, ok[2] & (core == 0)))
+        return tuple((slot, ok[slot]) for slot in range(3))
+
+    def pass_on(l):
         buf = R[f"buf{l}"]
-        for slot in range(3):
-            ok = facts[l][4][slot]
-            if l == 2:
-                direct = {0: core == 0, 1: core >= 0, 2: core == 1}[slot]
-
-                @pl.when(ok & direct)
-                def _(l=l, slot=slot, buf=buf):
-                    arrived(buf.at[slot], R[f"rs{l}"].at[slot])
-                    if slot != 1:
-                        relay(l, slot).start()
-            else:
-                @pl.when(ok)
-                def _(l=l, slot=slot, buf=buf):
-                    arrived(buf.at[core, slot], R[f"rs{l}"].at[slot])
-                    relay(l, slot).start()
+        for slot, ok in relays_out(l):
+            if l == 2 and slot == 1:
+                continue
+
+            @pl.when(ok)
+            def _(slot=slot):
+                mine = buf.at[slot] if l == 2 else buf.at[core, slot]
+                arrived(mine, R[f"rs{l}"].at[slot])
+                relay(l, slot).start()
+
+    def received(l):
+        buf = R[f"buf{l}"]
+        for slot, ok in relays_in(l):
+            @pl.when(ok)
+            def _(slot=slot):
+                theirs = buf.at[slot] if l == 2 else buf.at[other, slot]
+                arrived(theirs, R[f"yr{l}"].at[slot])
 
     @pl.when(has_left)
     def _():
@@ -286,6 +312,21 @@
         for name, at in (("fk", 0), ("fv", feats)):
             part = jnp.dot(pool1, R[name][side], preferred_element_type=jnp.float32)
             near[half * (1 + side) : half * (2 + side), at : at + feats] = part.astype(jnp.bfloat16)
+
+    near_at = pl.ds(pl.multiple_of(core * 3 * half, half), half)
+    quart = half // 2
+    pool4 = pool_matrix(quart, BLOCK, 4).astype(jnp.bfloat16)
+    pool2 = pool_matrix(quart, half, 2).astype(jnp.bfloat16)
+    for name, at in (("fk", 0), ("fv", feats)):
+        fine_part = jnp.dot(pool4, R[name][core], preferred_element_type=jnp.float32)
+        near_part = jnp.dot(pool2, near[near_at, at : at + feats], preferred_element_type=jnp.float32)
+        for part, place in ((near_part, core), (fine_part, other)):
+            rows = pl.ds(pl.multiple_of(place * quart, quart), quart)
+            R["stage"][rows, at : at + feats] = part.astype(jnp.bfloat16)
+
+    @pl.when(has_far)
+    def _():
+        relay(2, 1).start()
 
     gone_left = jnp.where(has_left, 0.0, NEVER).astype(jnp.float32)
     gone_right = jnp.where(has_right, 0.0, NEVER).astype(jnp.float32)
@@ -309,32 +350,18 @@
             for i in range(3):
                 fine[i, rows, ls] = both[i]
         m, z, o = attend(R["qp"][0:BLOCK, ls], near[:, ls], near[:, vs], R["bias"][...])
-        R["first"][0, :, ls] = m + LOG_TWO
-        R["first"][1, :, ls] = z
-        R["first"][2, :, ls] = o
+        R["terms1"][0, :, ls] = m + LOG_TWO
+        R["terms1"][1, :, ls] = z
+        R["terms1"][2, :, ls] = o
         return carry
 
     lax.fori_loop(0, plan.pairs, beside, 0, unroll=2)
 
-    for l in reversed(plan.deep):
-        buf = R[f"buf{l}"]
-        for slot in range(3):
-            ok = facts[l][4][slot]
-            if l == 2:
-                if slot == 1:
-                    continue
-
-                @pl.when(ok & (core == (1 if slot == 0 else 0)))
-                def _(slot=slot, buf=buf):
-                    arrived(buf.at[slot], R["yr2"].at[slot])
-            else:
-                @pl.when(ok)
-                def _(l=l, slot=slot, buf=buf):
-                    arrived(buf.at[other, slot], R[f"yr{l}"].at[slot])
+    def key_count(l):
+        return 3 * plan.padded[l] * (1 if l == 2 else 2 * plan.half_chips(l))
 
     def deep_bias(l):
-        slots = R[f"buf{l}"].shape[:-1]
-        width = math.prod(slots)
+        width = key_count(l)
         per_slot = plan.padded[l] * (1 if l == 2 else plan.half_chips(l))
         c = lax.broadcasted_iota(jnp.int32, (1, width), 1)
         slot = lax.rem(c // per_slot, 3)
@@ -344,9 +371,38 @@
             bias = jnp.where(lax.rem(c, plan.padded[l]) < plan.rows[l], bias, NEVER)
         return bias
 
-    def deepest(hp, carry):
+    def deep_level(l):
+        bias = deep_bias(l)
+        buf = R[f"buf{l}"]
+        width = key_count(l)
+        at = (slice(None),) * (len(buf.shape) - 1)
+
+        def body(hp, carry):
+            ls = lanes(hp)
+            if plan.packed(l):
+                block = buf[at + (ls,)].astype(jnp.float32)
+                keys = block[:, :, :, :8].reshape(width, LANES).astype(jnp.bfloat16)
+                values = block[:, :, :, 8:].reshape(width, LANES).astype(jnp.bfloat16)
+            else:
+                keys = buf[at + (ls,)].reshape(width, LANES)
+                values = buf[at + (lanes(hp, feats),)].reshape(width, LANES)
+            q = R["qp"][plan.offset[l] : plan.offset[l] + plan.padded[l], ls]
+            m, z, o = attend(q, keys, values, bias)
+            R[f"terms{l}"][0, :, ls] = m + l * LOG_TWO
+            R[f"terms{l}"][1, :, ls] = z
+            R[f"terms{l}"][2, :, ls] = o
+            return carry
+
+        lax.fori_loop(0, plan.pairs, body, 0, unroll=2)
+
+    for l in reversed(plan.deep):
+        pass_on(l)
+    for l in reversed(plan.deep):
+        received(l)
+        deep_level(l)
+
+    def last(hp, carry):
         ls = lanes(hp)
-        vs = lanes(hp, feats)
 
         def widen(l, terms):
             wide = R[f"wide{l}"]
@@ -360,17 +416,7 @@
 
         current = None
         for l in reversed(plan.levels):
-            if l == 1:
-                terms = tuple(R["first"][i, :, ls] for i in range(3))
-            else:
-                buf = R[f"buf{l}"]
-                width = math.prod(buf.shape[:-1])
-                at = (slice(None),) * (len(buf.shape) - 1)
-                keys = buf[at + (ls,)].reshape(width, LANES).astype(jnp.bfloat16)
-                values = buf[at + (vs,)].reshape(width, LANES).astype(jnp.bfloat16)
-                q = R["qp"][plan.offset[l] : plan.offset[l] + plan.padded[l], ls]
-                m, z, o = attend(q, keys, values, deep_bias(l))
-                terms = (m + l * LOG_TWO, z, o)
+            terms = tuple(R[f"terms{l}"][i, :, ls] for i in range(3))
             current = terms if current is None else merge(current, terms)
             current = widen(l, current)
         fine = tuple(R["fine"][i, :, ls] for i in range(3))
@@ -378,18 +424,12 @@
         out_ref[:, ls] = (o / z).astype(jnp.bfloat16)
         return carry
 
-    lax.fori_loop(0, plan.pairs, deepest, 0, unroll=2)
+    lax.fori_loop(0, plan.pairs, last, 0, unroll=2)
 
     all_deep(lambda copy: copy.wait_send())
-    neighbour_copies(lambda copy: copy.wait_send())
+    neighbour_copies(lambda copy: copy.wait_send(), (0, 1, 2))
     for l in plan.deep:
-        for slot in range(3):
-            ok = facts[l][4][slot]
-            if l == 2:
-                if slot == 1:
-                    continue
-                ok = ok & (core == (0 if slot == 0 else 1))
-
+        for slot, ok in relays_out(l):
             @pl.when(ok)
             def _(l=l, slot=slot):
                 relay(l, slot).wait_send()
@@ -399,18 +439,20 @@
     f, length = plan.features, plan.length
     scratch = {}
     scratch["qp"] = pltpu.VMEM((plan.pooled_rows, f), jnp.float32)
+    sem = pltpu.SemaphoreType.DMA
     for l in plan.levels:
-        kind = plan.link_type(l)
-        scratch[f"send{l}"] = pltpu.VMEM((plan.padded[l], 2 * f), kind)
+        link = plan.link_shape(l)
+        scratch[f"send{l}"] = pltpu.VMEM(link, jnp.bfloat16)
+        scratch[f"terms{l}"] = pltpu.VMEM((3, plan.padded[l], f), jnp.float32)
         if l == 1:
             continue
-        sem = pltpu.SemaphoreType.DMA
         if l == 2:
-            scratch["buf2"] = pltpu.VMEM((3, plan.padded[2], 2 * f), kind)
+            scratch["buf2"] = pltpu.VMEM((3,) + link, jnp.bfloat16)
+            scratch["stage"] = pltpu.VMEM(link, jnp.bfloat16)
             scratch["ss2"] = sem((2, 1))
         else:
             m = plan.half_chips(l)
-            scratch[f"buf{l}"] = pltpu.VMEM((2, 3, m, plan.padded[l], 2 * f), kind)
+            scratch[f"buf{l}"] = pltpu.VMEM((2, 3, m) + link, jnp.bfloat16)
             scratch[f"ss{l}"] = sem((2, 2 * m))
         scratch[f"rs{l}"] = sem((3,))
         scratch[f"ys{l}"] = sem((3,))
@@ -421,7 +463,6 @@
     scratch["fs"] = pltpu.SemaphoreType.DMA((6,))
     scratch["fr"] = pltpu.SemaphoreType.DMA((6,))
     scratch["fine"] = pltpu.VMEM((3, length, f), jnp.float32)
-    scratch["first"] = pltpu.VMEM((3, BLOCK, f), jnp.float32)
     scratch["bias"] = pltpu.VMEM((BLOCK, 2 * BLOCK), jnp.float32)
     for l in plan.levels:
         scratch[f"wide{l}"] = pltpu.VMEM((plan.pairs, 3, 2 * plan.padded[l], LANES), jnp.float32)

time: 53.3 us -> 48.1 us (0.902)
  the two profiles are of different devices: /device:TPU:1 before, /device:TPU:11 now
where the time goes in v2:
time: 48.1 us; the launch traced here: 47.9 us
  Pallas kernels  46.2 us (96%)
  local copies, waits for them, and re-layouts  1.77 us (4%)
    pallas_call x1, Pallas kernels, shards(): pl.pallas_call(functools.partial(kernel, plan, names), out_shape=jax.Shap...  46.2 us
    unnamed x1, local copies, waits for them, and re-layouts  1.77 us

profile of v2, /device:TPU:11, one launch (start us, length us, event | category | flops | bytes accessed | tf_op | source)
XLA Modules:
  0.0 47.9 jit_solution(2764755050740004536)
XLA Ops:
  0.0 46.2 %hier_attention.1 = bf16[256,768]{1,0:T(8,128)(2,1)} custom-call(bf16[256,768]{1,0:T(8,128)(2,1)} %refs_0_.1, bf16[256,768]{1,0:T(8,128)(2,1)} %refs_1_.1, bf16[256,768]{1,0:T(8,128)(2,1)} %refs_2_.1), custom_call_target="tpu_custom_call" | custom-call | tf_op jit(solution)/shard_map/hier_attention/pallas_call | solution.py:470
  46.2 1.8 %copy.5 = bf16[256,768]{1,0:T(8,128)(2,1)} copy(bf16[256,768]{1,0:T(8,128)(2,1)} %hier_attention.1) | data formatting | bytes 786432

commit v3 on v2

--- a/solution.py
+++ b/solution.py
@@ -105,22 +105,31 @@
     sibling = device(2 * chip + other)
 
     barrier = pltpu.get_barrier_semaphore()
-
-    def greet(i, carry):
-        @pl.when(i != chip)
-        def _():
-            pl.semaphore_signal(barrier, inc=1, device_id=device(2 * i + core), device_id_type=MESH)
-
-        return carry
-
-    lax.fori_loop(0, plan.chips, greet, 0)
-    pl.semaphore_signal(barrier, inc=1, device_id=sibling, device_id_type=MESH)
+    bits = plan.chips.bit_length() - 1
+
+    def across(i):
+        mask = 2**i
+        flipped = jnp.where(lax.rem(lax.div(chip, mask), 2) == 1, chip - mask, chip + mask)
+        return device(2 * flipped + core)
+
     far = jnp.where(core == 0, pos - 1, pos + 1)
     has_far = (far >= 0) & (far < plan.devices)
+    pl.semaphore_signal(barrier, inc=1, device_id=sibling, device_id_type=MESH)
 
     @pl.when(has_far)
     def _():
         pl.semaphore_signal(barrier, inc=1, device_id=device(far), device_id_type=MESH)
+
+    for i in range(bits):
+        pl.semaphore_signal(barrier, inc=1, device_id=across(i), device_id_type=MESH)
+
+    def tell(i):
+        if i < bits:
+            pl.semaphore_signal(R["go"].at[i], inc=1, device_id=across(i), device_id_type=MESH)
+
+    def hear(i):
+        if i < bits:
+            pl.semaphore_wait(R["go"].at[i], 1)
 
     facts = {}
     for l in plan.deep:
@@ -155,7 +164,8 @@
         R["fv"][1] = jnp.zeros((BLOCK, feats), jnp.bfloat16)
         near[3 * half :] = jnp.zeros((half, 2 * feats), jnp.bfloat16)
 
-    pl.semaphore_wait(barrier, plan.chips + jnp.where(has_far, 1, 0))
+    pl.semaphore_wait(barrier, bits + 1 + jnp.where(has_far, 1, 0))
+    tell(0)
 
     def remote(src, dst, send_sem, recv_sem, target):
         return pltpu.make_async_remote_copy(
@@ -200,6 +210,28 @@
         R[f"send{l}"][...] = jnp.concatenate(parts, axis=0).astype(jnp.bfloat16)
 
     neighbour_copies(lambda copy: copy.start(), (2,))
+
+    def lanes(hp, base=0):
+        return pl.ds(pl.multiple_of(base + hp * LANES, LANES), LANES)
+
+    def own(hp, carry):
+        ls = lanes(hp)
+        q = q_ref[:, ls].astype(jnp.float32) * 0.125
+        m, z, o = attend(q, k_ref[:, ls], v_ref[:, ls], None)
+        R["fine"][0, :, ls] = m
+        R["fine"][1, :, ls] = z
+        R["fine"][2, :, ls] = o
+        return carry
+
+    parts = 3
+    for i in range(parts):
+        hear(i)
+        tell(i + 1)
+        low, high = i * plan.pairs // parts, (i + 1) * plan.pairs // parts
+        lax.fori_loop(low, high, own, 0, unroll=True)
+    for i in range(parts, bits):
+        hear(i)
+        tell(i + 1)
 
     def deep_copies(l, t, act):
         J, b, left_ok, right_ok, _ = facts[l]
@@ -226,7 +258,7 @@
                 act(remote(send, dst, ss.at[side, t], rs.at[slot], target))
 
     def all_deep(act):
-        for l in reversed(plan.deep):
+        for l in plan.deep:
             if l == 2:
                 deep_copies(l, 0, act)
             else:
@@ -237,20 +269,6 @@
                 lax.fori_loop(0, 2 * plan.half_chips(l), body, 0)
 
     all_deep(lambda copy: copy.start())
-
-    def lanes(hp, base=0):
-        return pl.ds(pl.multiple_of(base + hp * LANES, LANES), LANES)
-
-    def own(hp, carry):
-        ls = lanes(hp)
-        q = q_ref[:, ls].astype(jnp.float32) * 0.125
-        m, z, o = attend(q, k_ref[:, ls], v_ref[:, ls], None)
-        R["fine"][0, :, ls] = m
-        R["fine"][1, :, ls] = z
-        R["fine"][2, :, ls] = o
-        return carry
-
-    lax.fori_loop(0, plan.pairs, own, 0, unroll=2)
 
     def arrived(ref, sem):
         pltpu.make_async_copy(ref, ref, sem).wait()
@@ -355,7 +373,7 @@
         R["terms1"][2, :, ls] = o
         return carry
 
-    lax.fori_loop(0, plan.pairs, beside, 0, unroll=2)
+    lax.fori_loop(0, plan.pairs, beside, 0, unroll=True)
 
     def key_count(l):
         return 3 * plan.padded[l] * (1 if l == 2 else 2 * plan.half_chips(l))
@@ -393,11 +411,12 @@
             R[f"terms{l}"][2, :, ls] = o
             return carry
 
-        lax.fori_loop(0, plan.pairs, body, 0, unroll=2)
-
-    for l in reversed(plan.deep):
-        pass_on(l)
-    for l in reversed(plan.deep):
+        lax.fori_loop(0, plan.pairs, body, 0, unroll=True)
+
+    pass_on(plan.deep[0])
+    for l in plan.deep:
+        if l < plan.top:
+            pass_on(l + 1)
         received(l)
         deep_level(l)
 
@@ -424,7 +443,7 @@
         out_ref[:, ls] = (o / z).astype(jnp.bfloat16)
         return carry
 
-    lax.fori_loop(0, plan.pairs, last, 0, unroll=2)
+    lax.fori_loop(0, plan.pairs, last, 0, unroll=True)
 
     all_deep(lambda copy: copy.wait_send())
     neighbour_copies(lambda copy: copy.wait_send(), (0, 1, 2))
@@ -460,6 +479,7 @@
     scratch["fk"] = pltpu.VMEM((2, BLOCK, f), jnp.bfloat16)
     scratch["fv"] = pltpu.VMEM((2, BLOCK, f), jnp.bfloat16)
     scratch["near"] = pltpu.VMEM((2 * BLOCK, 2 * f), jnp.bfloat16)
+    scratch["go"] = pltpu.SemaphoreType.REGULAR((max(1, plan.chips.bit_length() - 1),))
     scratch["fs"] = pltpu.SemaphoreType.DMA((6,))
     scratch["fr"] = pltpu.SemaphoreType.DMA((6,))
     scratch["fine"] = pltpu.VMEM((3, length, f), jnp.float32)

time: 48.1 us -> 41.7 us (0.87)
  the two profiles are of different devices: /device:TPU:11 before, /device:TPU:13 now
where the time goes in v3:
time: 41.7 us; the launch traced here: 41.5 us
  Pallas kernels  39.8 us (95%)
  local copies, waits for them, and re-layouts  1.77 us (4%)
    pallas_call x1, Pallas kernels, shards(): pl.pallas_call(functools.partial(kernel, plan, names), out_shape=jax.Shap...  39.8 us
    unnamed x1, local copies, waits for them, and re-layouts  1.77 us

profile of v3, /device:TPU:13, one launch (start us, length us, event | category | flops | bytes accessed | tf_op | source)
XLA Modules:
  0.0 41.5 jit_solution(16734654219907777809)
XLA Ops:
  0.0 39.8 %hier_attention.1 = bf16[256,768]{1,0:T(8,128)(2,1)} custom-call(bf16[256,768]{1,0:T(8,128)(2,1)} %refs_0_.1, bf16[256,768]{1,0:T(8,128)(2,1)} %refs_1_.1, bf16[256,768]{1,0:T(8,128)(2,1)} %refs_2_.1), custom_call_target="tpu_custom_call" | custom-call | tf_op jit(solution)/shard_map/hier_attention/pallas_call | solution.py:490
  39.8 1.8 %copy.5 = bf16[256,768]{1,0:T(8,128)(2,1)} copy(bf16[256,768]{1,0:T(8,128)(2,1)} %hier_attention.1) | data formatting | bytes 786432

commit v4 on v3

--- a/solution.py
+++ b/solution.py
@@ -13,6 +13,7 @@
 LANES = 128
 LOG_TWO = math.log(2.0)
 NEVER = -1e30
+ALL_HEADS_ROWS = 32
 MESH = pl.DeviceIdType.MESH
 
 
@@ -80,6 +81,33 @@
     return wide, z, o
 
 
+def attend_all(q, keys, values, bias):
+    n, feats = q.shape
+    w = keys.shape[0]
+    head_dim = feats // HEADS
+    row = lax.broadcasted_iota(jnp.int32, (HEADS * n, feats), 0)
+    lane = lax.broadcasted_iota(jnp.int32, (HEADS * n, feats), 1)
+    tall = jnp.concatenate([q] * HEADS, axis=0)
+    tall = jnp.where(row // n == lane // head_dim, tall, 0.0).astype(jnp.bfloat16)
+    s = lax.dot_general(tall, keys, (((1,), (1,)), ((), ())), preferred_element_type=jnp.float32)
+    s = s + bias
+    m = jnp.max(s, axis=1, keepdims=True)
+    p = jnp.exp(s - m).astype(jnp.bfloat16)
+    r = jnp.dot(p, values, preferred_element_type=jnp.float32)
+    z = jnp.dot(p, jnp.ones((w, LANES), jnp.bfloat16), preferred_element_type=jnp.float32)
+    first = lax.broadcasted_iota(jnp.int32, (n, LANES), 1) < LANES // 2
+    parts = []
+    for hp in range(feats // LANES):
+        a = slice(2 * hp * n, (2 * hp + 1) * n)
+        b = slice((2 * hp + 1) * n, (2 * hp + 2) * n)
+        ls = slice(hp * LANES, (hp + 1) * LANES)
+        wide = jnp.where(
+            first, jnp.broadcast_to(m[a], (n, LANES)), jnp.broadcast_to(m[b], (n, LANES))
+        )
+        parts.append((wide, jnp.where(first, z[a], z[b]), jnp.where(first, r[a, ls], r[b, ls])))
+    return parts
+
+
 def merge(one, two):
     top = jnp.maximum(one[0], two[0])
     a = jnp.exp(one[0] - top)
@@ -411,7 +439,22 @@
             R[f"terms{l}"][2, :, ls] = o
             return carry
 
-        lax.fori_loop(0, plan.pairs, body, 0, unroll=True)
+        if plan.padded[l] > ALL_HEADS_ROWS:
+            lax.fori_loop(0, plan.pairs, body, 0, unroll=True)
+            return
+        if plan.packed(l):
+            block = buf[...].astype(jnp.float32)
+            keys = block[:, :, :, :8].reshape(width, feats).astype(jnp.bfloat16)
+            values = block[:, :, :, 8:].reshape(width, feats).astype(jnp.bfloat16)
+        else:
+            keys = buf[at + (slice(0, feats),)].reshape(width, feats)
+            values = buf[at + (slice(feats, 2 * feats),)].reshape(width, feats)
+        q = R["qp"][plan.offset[l] : plan.offset[l] + plan.padded[l], :]
+        for hp, (m, z, o) in enumerate(attend_all(q, keys, values, bias)):
+            ls = slice(hp * LANES, (hp + 1) * LANES)
+            R[f"terms{l}"][0, :, ls] = m + l * LOG_TWO
+            R[f"terms{l}"][1, :, ls] = z
+            R[f"terms{l}"][2, :, ls] = o
 
     pass_on(plan.deep[0])
     for l in plan.deep:

time: 41.7 us -> 40.3 us (0.966)
  Pallas kernels: 39.8 us -> 38.4 us
    pallas_call x1, Pallas kernels: 39.8 us -> 38.4 us  [shards(): pl.pallas_call(functools.partial(kernel, plan, names), out_shape=jax.Shap...]
where the time goes in v4:
time: 40.3 us; the launch traced here: 40.1 us
  Pallas kernels  38.4 us (95%)
  local copies, waits for them, and re-layouts  1.77 us (4%)
    pallas_call x1, Pallas kernels, shards(): pl.pallas_call(functools.partial(kernel, plan, names), out_shape=jax.Shap...  38.4 us
    unnamed x1, local copies, waits for them, and re-layouts  1.77 us

profile of v4, /device:TPU:13, one launch (start us, length us, event | category | flops | bytes accessed | tf_op | source)
XLA Modules:
  0.0 40.1 jit_solution(17466608727184965703)
XLA Ops:
  0.0 38.4 %hier_attention.1 = bf16[256,768]{1,0:T(8,128)(2,1)} custom-call(bf16[256,768]{1,0:T(8,128)(2,1)} %refs_0_.1, bf16[256,768]{1,0:T(8,128)(2,1)} %refs_1_.1, bf16[256,768]{1,0:T(8,128)(2,1)} %refs_2_.1), custom_call_target="tpu_custom_call" | custom-call | tf_op jit(solution)/shard_map/hier_attention/pallas_call | solution.py:533
  38.4 1.8 %copy.5 = bf16[256,768]{1,0:T(8,128)(2,1)} copy(bf16[256,768]{1,0:T(8,128)(2,1)} %hier_attention.1) | data formatting | bytes 786432

commit v5 on v4

--- a/solution.py
+++ b/solution.py
@@ -204,7 +204,12 @@
     def neighbour_copies(act, which):
         send1 = R["send1"]
         fs, fr = R["fs"], R["fr"]
-        for side, ok, step in ((0, has_right, 1), (1, has_left, -1)):
+        for side, step, ok in (
+            (0, 1, has_right & (core == 1)),
+            (1, -1, has_left & (core == 0)),
+            (0, 1, core == 0),
+            (1, -1, core == 1),
+        ):
             @pl.when(ok)
             def _(side=side, step=step):
                 t = device(pos + step)
@@ -456,10 +461,9 @@
             R[f"terms{l}"][1, :, ls] = z
             R[f"terms{l}"][2, :, ls] = o
 
-    pass_on(plan.deep[0])
     for l in plan.deep:
-        if l < plan.top:
-            pass_on(l + 1)
+        pass_on(l)
+    for l in plan.deep:
         received(l)
         deep_level(l)
 

time: 40.3 us -> 39.5 us (0.980)
  the two profiles are of different devices: /device:TPU:13 before, /device:TPU:12 now
where the time goes in v5:
time: 39.5 us; the launch traced here: 39.3 us
  Pallas kernels  37.6 us (95%)
  local copies, waits for them, and re-layouts  1.77 us (4%)
    pallas_call x1, Pallas kernels, shards(): pl.pallas_call(functools.partial(kernel, plan, names), out_shape=jax.Shap...  37.6 us
    unnamed x1, local copies, waits for them, and re-layouts  1.77 us

profile of v5, /device:TPU:12, one launch (start us, length us, event | category | flops | bytes accessed | tf_op | source)
XLA Modules:
  0.0 39.3 jit_solution(8224333532241791241)
XLA Ops:
  0.0 37.6 %hier_attention.1 = bf16[256,768]{1,0:T(8,128)(2,1)} custom-call(bf16[256,768]{1,0:T(8,128)(2,1)} %refs_0_.1, bf16[256,768]{1,0:T(8,128)(2,1)} %refs_1_.1, bf16[256,768]{1,0:T(8,128)(2,1)} %refs_2_.1), custom_call_target="tpu_custom_call" | custom-call | tf_op jit(solution)/shard_map/hier_attention/pallas_call | solution.py:537
  37.6 1.8 %copy.5 = bf16[256,768]{1,0:T(8,128)(2,1)} copy(bf16[256,768]{1,0:T(8,128)(2,1)} %hier_attention.1) | data formatting | bytes 786432
